TPU v7x, 128 devices: a whole 4x4x4 slice. The times are simulated.
128 devices in a mesh: seq: 32 (over y, x, z_hi), grp: 4 (over z_lo, core).
Axes of the slice: x: 4, y: 4, z: 4 (z_hi: 2, z_lo: 2; z = z_hi * 2 + z_lo), core: 2. Of those that a mesh axis runs over, the one named last changes fastest.
Arguments:
- inputs: bfloat16 [4, 8192, 1536], P('grp', 'seq'), may hold values from -6 to 6
- cotangent: bfloat16 [4, 8192, 1536], P('grp', 'seq'), may hold values from -6 to 6
- filter_weight: bfloat16 [4608, 640], replicated, may hold values from -0.09375 to 0.09375
- projection_weight: bfloat16 [640, 1536], replicated, may hold values from -0.25 to 0.25
Outputs:
- input_gradient: bfloat16 [4, 8192, 1536], P('grp', 'seq')
- filter_gradient: float32 [4608, 640], P(('seq', 'grp'))
- projection_gradient: float32 [640, 1536], P(('seq', 'grp'))
All inputs are finite; a program needn't handle non-finite values.
Results may differ from a plain program's by a relative error of at most 0.0054.
Values may be sent and summed in bfloat16 or wider, within the bound.
A program may use at most 128 MiB of HBM per device.

v0:
```python
import jax
import jax.numpy as jnp
from jax import lax
from jax.sharding import PartitionSpec as P

DILATION = 64


def with_halo(block, sides, width):
    for axis, dim in sides:
        count = lax.axis_size(axis)
        forward = [(i, i + 1) for i in range(count - 1)]
        backward = [(target, source) for source, target in forward]
        low = lax.ppermute(
            lax.slice_in_dim(block, block.shape[dim] - width, None, axis=dim), axis, forward
        )
        high = lax.ppermute(lax.slice_in_dim(block, 0, width, axis=dim), axis, backward)
        block = jnp.concatenate([low, block, high], axis=dim)
    return block


def gelu_fwd(v):
    return jax.nn.gelu(v, approximate=True)


def gelu_slope(v):
    coeff = 0.7978845608028654
    inner = coeff * (v + 0.044715 * v * v * v)
    tanh_val = jnp.tanh(inner)
    return 0.5 * (1.0 + tanh_val) + 0.5 * v * (1.0 - tanh_val * tanh_val) * coeff * (
        1.0 + 3.0 * 0.044715 * v * v
    )


def sum_conv(term, total_rows):
    return lax.psum_scatter(
        term(
            jnp.int32(0),
            total_rows // lax.axis_size(("seq", "grp")) * lax.axis_size(("seq", "grp")),
        ),
        ("seq", "grp"),
        scatter_dimension=0,
        tiled=True,
    )


def sum_proj(term, total_rows):
    return lax.psum_scatter(
        term(
            jnp.int32(0),
            total_rows // lax.axis_size(("seq", "grp")) * lax.axis_size(("seq", "grp")),
        ),
        ("seq", "grp"),
        scatter_dimension=0,
        tiled=True,
    )


def shards(inputs, cotangent, filter_weight, projection_weight):
    positions = inputs.shape[1]
    chans = inputs.shape[2]
    hidden = projection_weight.shape[0]
    dist = DILATION
    count_all = inputs.shape[0] * lax.axis_size("grp") * positions * lax.axis_size("seq")
    gradient_scale = 1.0 / count_all**0.5
    act = gelu_fwd(inputs.astype(jnp.float32)).astype(jnp.bfloat16)
    padded = with_halo(act, (("seq", 1),), dist)
    taps = jnp.concatenate(
        [padded[:, :positions], act, padded[:, 2 * dist : 2 * dist + positions]], axis=-1
    )
    taps = taps.reshape(positions, 3 * chans)
    pre = jnp.dot(taps, filter_weight, preferred_element_type=jnp.float32)
    post = gelu_fwd(pre).astype(jnp.bfloat16)
    flat_up = cotangent.reshape(positions, chans)
    d_post = lax.dot_general(
        flat_up, projection_weight, (((1,), (1,)), ((), ())), preferred_element_type=jnp.float32
    )
    d_pre = (d_post * gelu_slope(pre)).astype(jnp.bfloat16)

    def proj_term(start, count):
        return (
            lax.dot_general(
                post, flat_up, (((0,), (0,)), ((), ())), preferred_element_type=jnp.float32
            )
            * gradient_scale
        )

    def conv_term(start, count):
        return (
            lax.dot_general(
                taps, d_pre, (((0,), (0,)), ((), ())), preferred_element_type=jnp.float32
            )
            * gradient_scale
        )

    projection_gradient = sum_proj(proj_term, hidden)
    filter_gradient = sum_conv(conv_term, 3 * chans)
    d_pre3 = d_pre.reshape(1, positions, hidden)
    rimmed = with_halo(d_pre3, (("seq", 1),), dist)
    pieces = [rimmed[0, 2 * dist : 2 * dist + positions], d_pre, rimmed[0, :positions]]
    d_act = jnp.zeros((positions, chans), jnp.float32)
    for k in range(3):
        d_act = d_act + lax.dot_general(
            pieces[k],
            filter_weight[k * chans : (k + 1) * chans],
            (((1,), (1,)), ((), ())),
            preferred_element_type=jnp.float32,
        )
    input_gradient = (
        cotangent.astype(jnp.float32)
        + d_act.reshape(1, positions, chans) * gelu_slope(inputs.astype(jnp.float32))
    ).astype(jnp.bfloat16)
    return (input_gradient, filter_gradient, projection_gradient)


def solution(mesh):
    in_specs = (P("grp", "seq", None), P("grp", "seq", None), P(), P())
    out_specs = (P("grp", "seq", None), P(("seq", "grp"), None), P(("seq", "grp"), None))
    return jax.shard_map(shards, mesh=mesh, in_specs=in_specs, out_specs=out_specs, check_vma=False)
```

profile of v0, /device:TPU:1, one launch (start us, length us, event | category | flops | bytes accessed | tf_op | source)
XLA Modules:
  0.0 615.9 jit_solution(16410891633331518602)
XLA Ops:
  7.2 1.8 fusion.19
  9.1 6.3 %collective-permute-start = (bf16[1,64,1536]{2,1,0:T(8,128)(2,1)S(1)}, bf16[1,64,1536]{2,1,0:T(8,128)(2,1)S(1)}, u32[]{:S(2)}, u32[]{:S(2)}) collective-permute-start(bf16[1,64,1536]{2,1,0:T(8,128)(2,1)S(1)} %get-tuple-element.3), channel_id=1, source_target_pairs={{0,4},{4,8},{8,12},{12,16},{16,20},{20,24},{24,28},{28,32},{32,36}... | collective-permute-start | bytes 589832 | tf_op jit(solution)/shard_map/ppermute | solution.py:14
  15.4 1.4 collective-permute-start.1
  16.9 2.1 collective-permute-done
  19.0 5.5 collective-permute-done.1
  24.4 4.8 fusion.44
  30.1 8.3 %convolution_multiply_fusion = f32[4608,640]{1,0:T(8,128)} fusion(bf16[256,640]{1,0:T(8,128)(2,1)S(1)} %fusion.27, bf16[1,64,1536]{2,1,0:T(8,128)(2,1)S(1)} %collective-permute-done.1, bf16[1,256,1536]{2,1,0:T(8,128)(2,1)S(1)} %fusion.19, bf16[1,64,1536]{2,1,0:T(8,128)(2,1)S(1)} %collective-permute-done), kind=kOutput, calls=%fused_computation | convolution fusion | flops 1524695040 | bytes 13303808 | tf_op jit(solution)/shard_map/dot_general | solution.py:90
  38.4 361.0 %fusion = f32[48,640]{1,0:T(8,128)S(1)} fusion(f32[4608,640]{1,0:T(8,128)} %convolution_multiply_fusion), kind=kCustom, calls=%all-reduce-scatter | all-reduce-scatter fusion | flops 3932161 | bytes 11919360
  399.5 1.3 collective-permute-start.10
  400.8 3.8 convolution_multiply_fusion.1
  405.9 1.9 collective-permute-start.3
  409.2 1.3 collective-permute-start.11
  410.5 1.3 collective-permute-start.12
  411.8 2.9 collective-permute-done.2
  416.0 1.3 collective-permute-start.14
  417.3 1.3 collective-permute-start.15
  418.6 1.3 collective-permute-start.16
  419.9 1.3 collective-permute-start.17
  421.2 25.0 %collective-permute-start.18 = (f32[48,640]{1,0:T(8,128)S(1)}, f32[48,640]{1,0:T(8,128)S(1)}, u32[]{:S(2)}, u32[]{:S(2)}) collective-permute-start(f32[48,640]{1,0:T(8,128)S(1)} %fusion), channel_id=1, source_target_pairs={{0,15},{1,16},{2,17},{3,18},{4,19},{5,20},{6,21},{7,22},{8,23},{9,... | collective-permute-start | bytes 368648
  446.2 4.6 collective-permute-start.19
  450.9 2.5 collective-permute-start.20
  453.4 5.2 collective-permute-start.21
  458.6 3.1 collective-permute-start.22
  461.7 2.7 collective-permute-start.23
  464.5 4.8 collective-permute-start.24
  469.2 1.9 collective-permute-start.25
  471.2 9.4 %collective-permute-start.26 = (f32[48,640]{1,0:T(8,128)S(1)}, f32[48,640]{1,0:T(8,128)S(1)}, u32[]{:S(2)}, u32[]{:S(2)}) collective-permute-start(f32[48,640]{1,0:T(8,128)S(1)} %fusion), channel_id=1, source_target_pairs={{0,23},{1,24},{2,25},{3,26},{4,27},{5,28},{6,29},{7,30},{8,31},{9,... | collective-permute-start | bytes 368648
  480.6 1.6 collective-permute-start.27
  482.2 2.2 collective-permute-start.28
  484.5 1.3 collective-permute-start.29
  485.8 3.7 collective-permute-start.30
  489.5 2.4 fusion.11
  491.9 2.7 collective-permute-start.31
  494.6 3.2 collective-permute-start.32
  497.8 1.3 collective-permute-start.33
  499.2 1.3 collective-permute-start.34
  501.2 2.1 collective-permute-start.4
  503.3 2.4 fusion.9
  505.7 1.3 collective-permute-start.5
  507.1 3.1 collective-permute-start.6
  510.1 6.2 %collective-permute-start.7 = (f32[48,640]{1,0:T(8,128)S(1)}, f32[48,640]{1,0:T(8,128)S(1)}, u32[]{:S(2)}, u32[]{:S(2)}) collective-permute-start(f32[48,640]{1,0:T(8,128)S(1)} %fusion), channel_id=1, source_target_pairs={{0,4},{1,5},{2,6},{3,7},{4,8},{5,9},{6,10},{7,11},{8,12},{9,13},{1... | collective-permute-start | bytes 368648
  516.4 3.0 collective-permute-start.8
  520.1 2.0 collective-permute-start.9
  522.1 4.1 fusion.5
  527.6 50.1 %concatenate.22 = f32[1572,640]{1,0:T(8,128)} concatenate(f32[36,640]{1,0:T(8,128)S(1)} %collective-permute-done.35, f32[48,640]{1,0:T(8,128)} %copy-done.15, f32[48,640]{1,0:T(8,128)} %copy-done.14, f32[48,640]{1,0:T(8,128)} %copy-done.13, f32[48,640]{1,0:T(8,128)} %copy-done.12, f32[48,640]{1,0:T(8,128)} %copy-done.11, f32[48,640]{1,0:T(8,128)} %copy-done.10, ...), dimensions={0} | concatenate | bytes 8048640
  577.7 1.6 constant_dynamic-slice_fusion
  579.2 28.3 %all-reduce.5.cloned.1.call-done = f32[640,1536]{1,0:T(8,128)} async-done(((f32[640,1536]{1,0:T(8,128)}), f32[640,1536]{1,0:T(8,128)}) %all-reduce.5.cloned.1.call-update) | async-done | bytes 3932176
  607.5 1.5 constant_dynamic-slice_fusion.1
  (84 shorter events, 7.7 us)
Async XLA Ops:
  7.2 22.0 %copy-start = (bf16[640,1536]{1,0:T(8,128)(2,1)S(1)}, bf16[640,1536]{1,0:T(8,128)(2,1)}, u32[]{:S(2)}) copy-start(bf16[640,1536]{1,0:T(8,128)(2,1)} %param.7) | copy-start | bytes 5898244
  7.2 600.3 %all-reduce.5.cloned.1.call-start = ((), (), s32[]{:S(2)}) async-start(), calls=%async_computation | async-start | bytes 7864320
  9.1 9.9 %collective-permute-start = (bf16[1,64,1536]{2,1,0:T(8,128)(2,1)S(1)}, bf16[1,64,1536]{2,1,0:T(8,128)(2,1)S(1)}, u32[]{:S(2)}, u32[]{:S(2)}) collective-permute-start(bf16[1,64,1536]{2,1,0:T(8,128)(2,1)S(1)} %get-tuple-element.3), channel_id=1, source_target_pairs={{0,4},{4,8},{8,12},{12,16},{16,20},{20,24},{24,28},{28,32},{32,36}... | collective-permute-start | bytes 589832 | tf_op jit(solution)/shard_map/ppermute | solution.py:14
  15.4 13.8 %copy-start.2 = (bf16[1,256,1536]{2,1,0:T(8,128)(2,1)S(1)}, bf16[1,256,1536]{2,1,0:T(8,128)(2,1)}, u32[]{:S(2)}) copy-start(bf16[1,256,1536]{2,1,0:T(8,128)(2,1)} %param.5) | copy-start | bytes 2359300
  15.4 9.0 %collective-permute-start.1 = (bf16[1,64,1536]{2,1,0:T(8,128)(2,1)S(1)}, bf16[1,64,1536]{2,1,0:T(8,128)(2,1)S(1)}, u32[]{:S(2)}, u32[]{:S(2)}) collective-permute-start(bf16[1,64,1536]{2,1,0:T(8,128)(2,1)S(1)} %get-tuple-element.4), channel_id=1, source_target_pairs={{4,0},{8,4},{12,8},{16,12},{20,16},{24,20},{28,24},{32,28},{36,32}... | collective-permute-start | bytes 589832 | tf_op jit(solution)/shard_map/ppermute | solution.py:17
  399.5 17.8 %collective-permute-start.10 = (f32[48,640]{1,0:T(8,128)S(1)}, f32[48,640]{1,0:T(8,128)S(1)}, u32[]{:S(2)}, u32[]{:S(2)}) collective-permute-start(f32[48,640]{1,0:T(8,128)S(1)} %fusion), channel_id=1, source_target_pairs={{0,7},{1,8},{2,9},{3,10},{4,11},{5,12},{6,13},{7,14},{8,15},{9,16}... | collective-permute-start | bytes 368648
  404.6 11.3 %collective-permute-start.35 = (f32[36,640]{1,0:T(8,128)S(1)}, f32[36,640]{1,0:T(8,128)S(1)}, u32[]{:S(2)}, u32[]{:S(2)}) collective-permute-start(f32[36,640]{1,0:T(8,128)S(1)} %slice.52), channel_id=1, source_target_pairs={{0,32},{1,33},{2,34},{3,35},{4,36},{5,37},{6,38},{7,39},{8,40},{9,... | collective-permute-start | bytes 276488
  405.9 4.5 collective-permute-start.3
  407.9 6.8 %collective-permute-start.2 = (bf16[1,64,640]{2,1,0:T(8,128)(2,1)S(1)}, bf16[1,64,640]{2,1,0:T(8,128)(2,1)}, u32[]{:S(2)}, u32[]{:S(2)}) collective-permute-start(bf16[1,64,640]{2,1,0:T(8,128)(2,1)S(1)} %get-tuple-element.5), channel_id=1, source_target_pairs={{4,0},{8,4},{12,8},{16,12},{20,16},{24,20},{28,24},{32,28},{36,32}... | collective-permute-start | bytes 245768 | tf_op jit(solution)/shard_map/ppermute | solution.py:17
  409.2 9.4 %collective-permute-start.11 = (f32[48,640]{1,0:T(8,128)S(1)}, f32[48,640]{1,0:T(8,128)S(1)}, u32[]{:S(2)}, u32[]{:S(2)}) collective-permute-start(f32[48,640]{1,0:T(8,128)S(1)} %fusion), channel_id=1, source_target_pairs={{0,8},{1,9},{2,10},{3,11},{4,12},{5,13},{6,14},{7,15},{8,16},{9,17... | collective-permute-start | bytes 368648
  410.5 9.4 %collective-permute-start.12 = (f32[48,640]{1,0:T(8,128)S(1)}, f32[48,640]{1,0:T(8,128)S(1)}, u32[]{:S(2)}, u32[]{:S(2)}) collective-permute-start(f32[48,640]{1,0:T(8,128)S(1)} %fusion), channel_id=1, source_target_pairs={{0,9},{1,10},{2,11},{3,12},{4,13},{5,14},{6,15},{7,16},{8,17},{9,1... | collective-permute-start | bytes 368648
  414.7 6.6 %collective-permute-start.13 = (f32[48,640]{1,0:T(8,128)S(1)}, f32[48,640]{1,0:T(8,128)S(1)}, u32[]{:S(2)}, u32[]{:S(2)}) collective-permute-start(f32[48,640]{1,0:T(8,128)S(1)} %fusion), channel_id=1, source_target_pairs={{0,10},{1,11},{2,12},{3,13},{4,14},{5,15},{6,16},{7,17},{8,18},{9,... | collective-permute-start | bytes 368648
  416.0 30.3 %collective-permute-start.14 = (f32[48,640]{1,0:T(8,128)S(1)}, f32[48,640]{1,0:T(8,128)S(1)}, u32[]{:S(2)}, u32[]{:S(2)}) collective-permute-start(f32[48,640]{1,0:T(8,128)S(1)} %fusion), channel_id=1, source_target_pairs={{0,11},{1,12},{2,13},{3,14},{4,15},{5,16},{6,17},{7,18},{8,19},{9,... | collective-permute-start | bytes 368648
  417.3 33.6 %collective-permute-start.15 = (f32[48,640]{1,0:T(8,128)S(1)}, f32[48,640]{1,0:T(8,128)S(1)}, u32[]{:S(2)}, u32[]{:S(2)}) collective-permute-start(f32[48,640]{1,0:T(8,128)S(1)} %fusion), channel_id=1, source_target_pairs={{0,12},{1,13},{2,14},{3,15},{4,16},{5,17},{6,18},{7,19},{8,20},{9,... | collective-permute-start | bytes 368648
  418.6 34.8 %collective-permute-start.16 = (f32[48,640]{1,0:T(8,128)S(1)}, f32[48,640]{1,0:T(8,128)S(1)}, u32[]{:S(2)}, u32[]{:S(2)}) collective-permute-start(f32[48,640]{1,0:T(8,128)S(1)} %fusion), channel_id=1, source_target_pairs={{0,13},{1,14},{2,15},{3,16},{4,17},{5,18},{6,19},{7,20},{8,21},{9,... | collective-permute-start | bytes 368648
  419.9 38.7 %collective-permute-start.17 = (f32[48,640]{1,0:T(8,128)S(1)}, f32[48,640]{1,0:T(8,128)S(1)}, u32[]{:S(2)}, u32[]{:S(2)}) collective-permute-start(f32[48,640]{1,0:T(8,128)S(1)} %fusion), channel_id=1, source_target_pairs={{0,14},{1,15},{2,16},{3,17},{4,18},{5,19},{6,20},{7,21},{8,22},{9,... | collective-permute-start | bytes 368648
  421.2 40.5 %collective-permute-start.18 = (f32[48,640]{1,0:T(8,128)S(1)}, f32[48,640]{1,0:T(8,128)S(1)}, u32[]{:S(2)}, u32[]{:S(2)}) collective-permute-start(f32[48,640]{1,0:T(8,128)S(1)} %fusion), channel_id=1, source_target_pairs={{0,15},{1,16},{2,17},{3,18},{4,19},{5,20},{6,21},{7,22},{8,23},{9,... | collective-permute-start | bytes 368648
  446.2 18.2 %collective-permute-start.19 = (f32[48,640]{1,0:T(8,128)S(1)}, f32[48,640]{1,0:T(8,128)S(1)}, u32[]{:S(2)}, u32[]{:S(2)}) collective-permute-start(f32[48,640]{1,0:T(8,128)S(1)} %fusion), channel_id=1, source_target_pairs={{0,16},{1,17},{2,18},{3,19},{4,20},{5,21},{6,22},{7,23},{8,24},{9,... | collective-permute-start | bytes 368648
  450.9 18.4 %collective-permute-start.20 = (f32[48,640]{1,0:T(8,128)S(1)}, f32[48,640]{1,0:T(8,128)S(1)}, u32[]{:S(2)}, u32[]{:S(2)}) collective-permute-start(f32[48,640]{1,0:T(8,128)S(1)} %fusion), channel_id=1, source_target_pairs={{0,17},{1,18},{2,19},{3,20},{4,21},{5,22},{6,23},{7,24},{8,25},{9,... | collective-permute-start | bytes 368648
  453.4 17.8 %collective-permute-start.21 = (f32[48,640]{1,0:T(8,128)S(1)}, f32[48,640]{1,0:T(8,128)}, u32[]{:S(2)}, u32[]{:S(2)}) collective-permute-start(f32[48,640]{1,0:T(8,128)S(1)} %fusion), channel_id=1, source_target_pairs={{0,18},{1,19},{2,20},{3,21},{4,22},{5,23},{6,24},{7,25},{8,26},{9,... | collective-permute-start | bytes 368648
  458.6 22.0 %collective-permute-start.22 = (f32[48,640]{1,0:T(8,128)S(1)}, f32[48,640]{1,0:T(8,128)}, u32[]{:S(2)}, u32[]{:S(2)}) collective-permute-start(f32[48,640]{1,0:T(8,128)S(1)} %fusion), channel_id=1, source_target_pairs={{0,19},{1,20},{2,21},{3,22},{4,23},{5,24},{6,25},{7,26},{8,27},{9,... | collective-permute-start | bytes 368648
  461.7 7.5 %copy-start.4 = (f32[48,640]{1,0:T(8,128)}, f32[48,640]{1,0:T(8,128)S(1)}, u32[]{:S(2)}) copy-start(f32[48,640]{1,0:T(8,128)S(1)} %collective-permute-done.18) | copy-start | bytes 368644
  461.7 20.5 %collective-permute-start.23 = (f32[48,640]{1,0:T(8,128)S(1)}, f32[48,640]{1,0:T(8,128)}, u32[]{:S(2)}, u32[]{:S(2)}) collective-permute-start(f32[48,640]{1,0:T(8,128)S(1)} %fusion), channel_id=1, source_target_pairs={{0,20},{1,21},{2,22},{3,23},{4,24},{5,25},{6,26},{7,27},{8,28},{9,... | collective-permute-start | bytes 368648
  464.5 6.7 %copy-start.5 = (f32[48,640]{1,0:T(8,128)}, f32[48,640]{1,0:T(8,128)S(1)}, u32[]{:S(2)}) copy-start(f32[48,640]{1,0:T(8,128)S(1)} %collective-permute-done.19) | copy-start | bytes 368644
  464.5 20.0 %collective-permute-start.24 = (f32[48,640]{1,0:T(8,128)S(1)}, f32[48,640]{1,0:T(8,128)}, u32[]{:S(2)}, u32[]{:S(2)}) collective-permute-start(f32[48,640]{1,0:T(8,128)S(1)} %fusion), channel_id=1, source_target_pairs={{0,21},{1,22},{2,23},{3,24},{4,25},{5,26},{6,27},{7,28},{8,29},{9,... | collective-permute-start | bytes 368648
  469.2 16.6 %collective-permute-start.25 = (f32[48,640]{1,0:T(8,128)S(1)}, f32[48,640]{1,0:T(8,128)}, u32[]{:S(2)}, u32[]{:S(2)}) collective-permute-start(f32[48,640]{1,0:T(8,128)S(1)} %fusion), channel_id=1, source_target_pairs={{0,22},{1,23},{2,24},{3,25},{4,26},{5,27},{6,28},{7,29},{8,30},{9,... | collective-permute-start | bytes 368648
  471.2 20.7 %collective-permute-start.26 = (f32[48,640]{1,0:T(8,128)S(1)}, f32[48,640]{1,0:T(8,128)S(1)}, u32[]{:S(2)}, u32[]{:S(2)}) collective-permute-start(f32[48,640]{1,0:T(8,128)S(1)} %fusion), channel_id=1, source_target_pairs={{0,23},{1,24},{2,25},{3,26},{4,27},{5,28},{6,29},{7,30},{8,31},{9,... | collective-permute-start | bytes 368648
  480.6 14.1 %collective-permute-start.27 = (f32[48,640]{1,0:T(8,128)S(1)}, f32[48,640]{1,0:T(8,128)S(1)}, u32[]{:S(2)}, u32[]{:S(2)}) collective-permute-start(f32[48,640]{1,0:T(8,128)S(1)} %fusion), channel_id=1, source_target_pairs={{0,24},{1,25},{2,26},{3,27},{4,28},{5,29},{6,30},{7,31},{8,32},{9,... | collective-permute-start | bytes 368648
  482.2 15.6 %collective-permute-start.28 = (f32[48,640]{1,0:T(8,128)S(1)}, f32[48,640]{1,0:T(8,128)S(1)}, u32[]{:S(2)}, u32[]{:S(2)}) collective-permute-start(f32[48,640]{1,0:T(8,128)S(1)} %fusion), channel_id=1, source_target_pairs={{0,25},{1,26},{2,27},{3,28},{4,29},{5,30},{6,31},{7,32},{8,33},{9,... | collective-permute-start | bytes 368648
  484.5 14.6 %collective-permute-start.29 = (f32[48,640]{1,0:T(8,128)S(1)}, f32[48,640]{1,0:T(8,128)S(1)}, u32[]{:S(2)}, u32[]{:S(2)}) collective-permute-start(f32[48,640]{1,0:T(8,128)S(1)} %fusion), channel_id=1, source_target_pairs={{0,26},{1,27},{2,28},{3,29},{4,30},{5,31},{6,32},{7,33},{8,34},{9,... | collective-permute-start | bytes 368648
  485.8 14.7 %collective-permute-start.30 = (f32[48,640]{1,0:T(8,128)S(1)}, f32[48,640]{1,0:T(8,128)S(1)}, u32[]{:S(2)}, u32[]{:S(2)}) collective-permute-start(f32[48,640]{1,0:T(8,128)S(1)} %fusion), channel_id=1, source_target_pairs={{0,27},{1,28},{2,29},{3,30},{4,31},{5,32},{6,33},{7,34},{8,35},{9,... | collective-permute-start | bytes 368648
  491.9 30.2 %copy-start.1 = (bf16[1,256,1536]{2,1,0:T(8,128)(2,1)S(1)}, bf16[1,256,1536]{2,1,0:T(8,128)(2,1)}, u32[]{:S(2)}) copy-start(bf16[1,256,1536]{2,1,0:T(8,128)(2,1)} %param.4) | copy-start | bytes 2359300
  491.9 30.2 %copy-start.3 = (bf16[1,256,1536]{2,1,0:T(8,128)(2,1)S(1)}, bf16[1,256,1536]{2,1,0:T(8,128)(2,1)}, u32[]{:S(2)}) copy-start(bf16[1,256,1536]{2,1,0:T(8,128)(2,1)} %param.5) | copy-start | bytes 2359300
  491.9 8.6 %copy-start.7 = (f32[48,640]{1,0:T(8,128)}, f32[48,640]{1,0:T(8,128)S(1)}, u32[]{:S(2)}) copy-start(f32[48,640]{1,0:T(8,128)S(1)} %collective-permute-done.26) | copy-start | bytes 368644
  491.9 13.8 %collective-permute-start.31 = (f32[48,640]{1,0:T(8,128)S(1)}, f32[48,640]{1,0:T(8,128)S(1)}, u32[]{:S(2)}, u32[]{:S(2)}) collective-permute-start(f32[48,640]{1,0:T(8,128)S(1)} %fusion), channel_id=1, source_target_pairs={{0,28},{1,29},{2,30},{3,31},{4,32},{5,33},{6,34},{7,35},{8,36},{9,... | collective-permute-start | bytes 368648
  494.6 5.8 copy-start.8
  494.6 12.4 %collective-permute-start.32 = (f32[48,640]{1,0:T(8,128)S(1)}, f32[48,640]{1,0:T(8,128)S(1)}, u32[]{:S(2)}, u32[]{:S(2)}) collective-permute-start(f32[48,640]{1,0:T(8,128)S(1)} %fusion), channel_id=1, source_target_pairs={{0,29},{1,30},{2,31},{3,32},{4,33},{5,34},{6,35},{7,36},{8,37},{9,... | collective-permute-start | bytes 368648
  497.8 12.3 %collective-permute-start.33 = (f32[48,640]{1,0:T(8,128)S(1)}, f32[48,640]{1,0:T(8,128)S(1)}, u32[]{:S(2)}, u32[]{:S(2)}) collective-permute-start(f32[48,640]{1,0:T(8,128)S(1)} %fusion), channel_id=1, source_target_pairs={{0,30},{1,31},{2,32},{3,33},{4,34},{5,35},{6,36},{7,37},{8,38},{9,... | collective-permute-start | bytes 368648
  499.2 17.2 %collective-permute-start.34 = (f32[48,640]{1,0:T(8,128)S(1)}, f32[48,640]{1,0:T(8,128)S(1)}, u32[]{:S(2)}, u32[]{:S(2)}) collective-permute-start(f32[48,640]{1,0:T(8,128)S(1)} %fusion), channel_id=1, source_target_pairs={{0,31},{1,32},{2,33},{3,34},{4,35},{5,36},{6,37},{7,38},{8,39},{9,... | collective-permute-start | bytes 368648
  501.2 18.2 %collective-permute-start.4 = (f32[48,640]{1,0:T(8,128)S(1)}, f32[48,640]{1,0:T(8,128)S(1)}, u32[]{:S(2)}, u32[]{:S(2)}) collective-permute-start(f32[48,640]{1,0:T(8,128)S(1)} %fusion), channel_id=1, source_target_pairs={{0,1},{1,2},{2,3},{3,4},{4,5},{5,6},{6,7},{7,8},{8,9},{9,10},{10,1... | collective-permute-start | bytes 368648
  505.7 13.6 %copy-start.12 = (f32[48,640]{1,0:T(8,128)}, f32[48,640]{1,0:T(8,128)S(1)}, u32[]{:S(2)}) copy-start(f32[48,640]{1,0:T(8,128)S(1)} %collective-permute-done.31) | copy-start | bytes 368644
  505.7 20.5 %collective-permute-start.5 = (f32[48,640]{1,0:T(8,128)S(1)}, f32[48,640]{1,0:T(8,128)S(1)}, u32[]{:S(2)}, u32[]{:S(2)}) collective-permute-start(f32[48,640]{1,0:T(8,128)S(1)} %fusion), channel_id=1, source_target_pairs={{0,2},{1,3},{2,4},{3,5},{4,6},{5,7},{6,8},{7,9},{8,10},{9,11},{10,... | collective-permute-start | bytes 368648
  507.0 12.3 %copy-start.13 = (f32[48,640]{1,0:T(8,128)}, f32[48,640]{1,0:T(8,128)S(1)}, u32[]{:S(2)}) copy-start(f32[48,640]{1,0:T(8,128)S(1)} %collective-permute-done.32) | copy-start | bytes 368644
  507.1 19.1 %collective-permute-start.6 = (f32[48,640]{1,0:T(8,128)S(1)}, f32[48,640]{1,0:T(8,128)S(1)}, u32[]{:S(2)}, u32[]{:S(2)}) collective-permute-start(f32[48,640]{1,0:T(8,128)S(1)} %fusion), channel_id=1, source_target_pairs={{0,3},{1,4},{2,5},{3,6},{4,7},{5,8},{6,9},{7,10},{8,11},{9,12},{10... | collective-permute-start | bytes 368648
  510.1 9.3 %copy-start.14 = (f32[48,640]{1,0:T(8,128)}, f32[48,640]{1,0:T(8,128)S(1)}, u32[]{:S(2)}) copy-start(f32[48,640]{1,0:T(8,128)S(1)} %collective-permute-done.33) | copy-start | bytes 368644
  510.1 16.1 %collective-permute-start.7 = (f32[48,640]{1,0:T(8,128)S(1)}, f32[48,640]{1,0:T(8,128)S(1)}, u32[]{:S(2)}, u32[]{:S(2)}) collective-permute-start(f32[48,640]{1,0:T(8,128)S(1)} %fusion), channel_id=1, source_target_pairs={{0,4},{1,5},{2,6},{3,7},{4,8},{5,9},{6,10},{7,11},{8,12},{9,13},{1... | collective-permute-start | bytes 368648
  516.4 9.8 %collective-permute-start.8 = (f32[48,640]{1,0:T(8,128)S(1)}, f32[48,640]{1,0:T(8,128)S(1)}, u32[]{:S(2)}, u32[]{:S(2)}) collective-permute-start(f32[48,640]{1,0:T(8,128)S(1)} %fusion), channel_id=1, source_target_pairs={{0,5},{1,6},{2,7},{3,8},{4,9},{5,10},{6,11},{7,12},{8,13},{9,14},{... | collective-permute-start | bytes 368648
  520.1 7.5 %collective-permute-start.9 = (f32[48,640]{1,0:T(8,128)S(1)}, f32[48,640]{1,0:T(8,128)}, u32[]{:S(2)}, u32[]{:S(2)}) collective-permute-start(f32[48,640]{1,0:T(8,128)S(1)} %fusion), channel_id=1, source_target_pairs={{0,6},{1,7},{2,8},{3,9},{4,10},{5,11},{6,12},{7,13},{8,14},{9,15},... | collective-permute-start | bytes 368648
  (10 other events, 13.0 us)
Sparse Core Ops, SparseCore 0:
  406.0 201.4 all-reduce.4
where the time goes:
time: 619 us; the launch traced here: 616 us
  blocking collectives  361 us (58%)
  starting transfers between devices  117 us (19%)
  local copies, waits for them, and re-layouts  55.9 us (9%)
  waiting for transfers between devices  38.8 us (6%)
  matrix products  26.6 us (4%)
  between operations  14.7 us (2%)
    unnamed x1, blocking collectives  361 us
    unnamed x33, starting transfers between devices  106 us
    unnamed x46, local copies, waits for them, and re-layouts  55.9 us
    unnamed x34, waiting for transfers between devices  28.4 us
  transfers between devices with their start and end apart: 37, of which 4 were waited for; matrix products, arithmetic and copies ran while one was open for 10% of the time, Pallas kernels for 0%

commit v1 on v0

v1 whole, which is shorter than its diff:
```python
import jax
import jax.numpy as jnp
from jax import lax
from jax.experimental import pallas as pl
from jax.experimental.pallas import tpu as pltpu
from jax.sharding import PartitionSpec as P

MESH = pl.DeviceIdType.MESH
BF, F32 = jnp.bfloat16, jnp.float32
D = 64
T = 256
C = 1536
H = 640
RA, RB = 1600, 1152
COEFF = 0.7978845608028654
NT = (((1,), (1,)), ((), ()))

S_HALO = 0
S_DZ = 2
S_SIB = 4
S_P1 = 12
S_P2 = 30
S_P3 = 39
N_SEM = 63


def tanh_of(v):
    return jnp.tanh(COEFF * (v + 0.044715 * (v * v * v)))


def slope(v, t):
    return 0.5 * (1.0 + t) + 0.5 * v * (1.0 - t * t) * COEFF * (1.0 + 3.0 * 0.044715 * v * v)


def dot(a, b):
    return jnp.dot(a, b, preferred_element_type=F32)


def dot_nt(a, b):
    return lax.dot_general(a, b, NT, preferred_element_type=F32)


def kernel(x_hbm, cot_hbm, fw_hbm, pw_hbm, ig_hbm, fo_ref, po_ref,
           xe, ue, ut, cot, fw, pw, z_ref, dg_ref, g_ref, gt, dz, dzx, dw,
           pa, pb, pc, rla, rlb, rlc, rfa, rfb, rfc,
           sa, qa, qb, qc, rqa, rqb, rqc, s2a, s2b, s2c, ta, tb, tc, rta, rtb, rtc,
           ig, lsem, ssem, rsem):
    seq, grp = lax.axis_index("seq"), lax.axis_index("grp")
    y, x, z, c = seq // 8, (seq // 2) % 4, (seq % 2) * 2 + grp // 2, grp % 2
    o = 1 - c

    def dev(xx, yy, zz, cc):
        return (yy * 8 + xx * 2 + zz // 2, (zz % 2) * 2 + cc)

    def at(axis, d, cc):
        xx = (x + d) % 4 if axis == "x" else x
        yy = (y + d) % 4 if axis == "y" else y
        zz = (z + d) % 4 if axis == "z" else z
        return dev(xx, yy, zz, cc)

    sibling = (seq, lax.rem(grp, 2) * (-2) + 1 + grp)
    pos = {"x": x, "y": y, "z": z}
    has_prev, has_next = seq > 0, seq < 31

    def remote(src, dst, sem, device):
        return pltpu.make_async_remote_copy(
            src_ref=src, dst_ref=dst, send_sem=ssem.at[sem[0]], recv_sem=rsem.at[sem[1]],
            device_id=device, device_id_type=MESH)

    def local(src, dst, i):
        return pltpu.make_async_copy(src, dst, lsem.at[i])

    load_x = local(x_hbm.at[0], xe.at[pl.ds(D, T)], 0)
    load_f = [local(fw_hbm.at[pl.ds(C * k, C)], fw.at[pl.ds(C * k, C)], 1 + k) for k in range(3)]
    load_c = local(cot_hbm.at[0], cot.at[pl.ds(0, T)], 4)
    load_p = local(pw_hbm, pw, 5)
    load_x.start()
    load_f[1].start()
    load_f[0].start()
    load_f[2].start()
    load_c.start()
    load_p.start()

    barrier = pltpu.get_barrier_semaphore()

    def greet(device):
        pl.semaphore_signal(barrier, inc=1, device_id=device, device_id_type=MESH)

    greet(sibling)
    for axis in ("x", "y", "z"):
        for d in (1, 2, 3):
            for cc in (0, 1):
                greet(at(axis, d, cc))
    nxt, prv = (seq + 1, grp), (seq - 1, grp)

    @pl.when(has_next)
    def _():
        greet(nxt)

    @pl.when(has_prev)
    def _():
        greet(prv)

    pl.semaphore_wait(barrier, 19 + has_prev.astype(jnp.int32) + has_next.astype(jnp.int32))

    halo_up = remote(x_hbm.at[0, pl.ds(T - D, D)], xe.at[pl.ds(0, D)], (S_HALO, S_HALO), nxt)
    halo_dn = remote(x_hbm.at[0, pl.ds(0, D)], xe.at[pl.ds(D + T, D)], (S_HALO + 1, S_HALO + 1), prv)
    dz_up = remote(dzx.at[pl.ds(T, D)], dzx.at[pl.ds(0, D)], (S_DZ, S_DZ), nxt)
    dz_dn = remote(dzx.at[pl.ds(D, D)], dzx.at[pl.ds(D + T, D)], (S_DZ + 1, S_DZ + 1), prv)

    @pl.when(has_next)
    def _():
        halo_up.start()

    @pl.when(has_prev)
    def _():
        halo_dn.start()

    sib_c = remote(cot_hbm.at[0], cot.at[pl.ds(T, T)], (S_SIB, S_SIB), sibling)
    sib_u = [remote(ut.at[0, i], ut.at[1, i], (S_SIB + 1 + i, S_SIB + 1 + i), sibling) for i in range(4)]
    sib_g = remote(gt.at[0], gt.at[1], (S_SIB + 5, S_SIB + 5), sibling)
    sib_d = remote(dz.at[0], dz.at[1], (S_SIB + 6, S_SIB + 6), sibling)
    sib_c.start()

    def act(start, rows):
        v = xe[pl.ds(start, rows)].astype(F32)
        ue[pl.ds(start, rows)] = (0.5 * v * (1.0 + tanh_of(v))).astype(BF)

    load_x.wait()

    @pl.loop(0, T // 32)
    def _(i):
        act(pl.multiple_of(D + i * 32, 32), 32)

    ut[0, 0] = ue[128:256].T
    ut[0, 2] = jnp.concatenate([ue[64:128], ue[256:320]], axis=0).T
    sib_u[0].start()
    sib_u[2].start()

    load_f[1].wait()
    z_ref[...] = dot(ue[64:320], fw[C:2 * C])
    load_f[0].wait()
    z_ref[64:256] += dot(ue[64:256], fw[0:C])
    load_f[2].wait()
    z_ref[0:192] += dot(ue[128:320], fw[2 * C:3 * C])
    load_c.wait()
    load_p.wait()
    dg_ref[...] = dot_nt(cot[0:T], pw[...])

    @pl.when(has_prev)
    def _():
        halo_up.wait_recv()
        act(0, 32)
        act(32, 32)

    @pl.when(jnp.logical_not(has_prev))
    def _():
        ue[0:D] = jnp.zeros((D, C), BF)

    @pl.when(has_next)
    def _():
        halo_dn.wait_recv()
        act(D + T, 32)
        act(D + T + 32, 32)

    @pl.when(jnp.logical_not(has_next))
    def _():
        ue[D + T:D + T + D] = jnp.zeros((D, C), BF)

    z_ref[0:64] += dot(ue[0:64], fw[0:C])
    z_ref[192:256] += dot(ue[320:384], fw[2 * C:3 * C])
    ut[0, 1] = ue[0:128].T
    ut[0, 3] = ue[256:384].T
    sib_u[1].start()
    sib_u[3].start()

    @pl.loop(0, T // 32)
    def _(i):
        rows = pl.ds(pl.multiple_of(i * 32, 32), 32)
        v = z_ref[rows]
        t = tanh_of(v)
        g_ref[rows] = (0.5 * v * (1.0 + t)).astype(BF)
        d = (dg_ref[rows] * slope(v, t)).astype(BF)
        dz[0, rows] = d
        dzx[pl.ds(pl.multiple_of(D + i * 32, 32), 32)] = d

    gt[0] = g_ref[...].T
    sib_g.start()
    sib_d.start()

    @pl.when(has_next)
    def _():
        dz_up.start()

    @pl.when(has_prev)
    def _():
        dz_dn.start()

    rings = {
        "A": ("y", lambda j, h: pa.at[j, pl.ds(RA // 2 * h, RA // 2)], rla, rfa, S_P1),
        "B": ("x", lambda j, h: pb.at[j, pl.ds(2 * h, 2)], rlb, rfb, S_P1 + 6),
        "C": ("z", lambda j, h: pc.at[j, pl.ds(2 * h, 2)], rlc, rfc, S_P1 + 12),
    }

    def ring(part):
        axis, chunk, rl, rf, sem = rings[part]
        i = pos[axis]
        up, far, dn = (i + 1) % 4, (i + 2) % 4, (i + 3) % 4
        out = []
        for k, (near, h, to) in enumerate(((up, 0, 1), (dn, 1, 3))):
            who = at(axis, to, c)
            s = sem + 3 * k
            out.append((
                remote(chunk(far, h), rl.at[k], (s, s), who),
                remote(chunk(near, 1 - h), rf.at[k, 0], (s + 1, s + 1), who),
                remote(chunk(near, h), rf.at[k, 1], (s + 2, s + 2), who),
                chunk(near, h), rl.at[k]))
        return out

    steps = {part: ring(part) for part in rings}

    def ring_start(part):
        for which in (0, 1):
            for k in (0, 1):
                steps[part][k][which].start()

    def ring_relay(part):
        for k in (0, 1):
            first, _, second, mine, came = steps[part][k]
            first.wait_recv()
            mine[...] = (mine[...].astype(F32) + came[...].astype(F32)).astype(BF)
            second.start()

    def ring_end(part):
        for k in (0, 1):
            steps[part][k][1].wait_recv()
            steps[part][k][2].wait_recv()

    sib_g.wait_recv()
    sib_c.wait_recv()

    @pl.loop(0, jnp.where(c == 0, 1, 5))
    def _(i):
        col = pl.multiple_of(256 * (i + c), 256)
        acc = dot(gt[0], cot[0:T, pl.ds(col, 256)]) + dot(gt[1], cot[T:2 * T, pl.ds(col, 256)])
        for j in range(4):
            for b in range(2):
                pa[j, pl.ds(pl.multiple_of(320 * i + 160 * b, 160), 160)] = (
                    acc[160 * j:160 * (j + 1), 128 * b:128 * (b + 1)].astype(BF))

    @pl.when(c == 1)
    def _():
        ring_start("A")

    sib_d.wait_recv()
    order = ((2, 3, 0, 1), (1, 2, 0, 3), (0, 1, 2, 3))
    col = pl.multiple_of(256 * c, 256)
    for k in range(3):
        for s in range(2):
            for b in range(4):
                src = pl.ds(64 * order[k][b], 64)
                dst = pl.ds(256 * s + 64 * b, 64)
                dw[k, dst, 0:256] = dz[s, src, pl.ds(col, 256)]
                dw[k, dst, 256:384] = dz[s, src, 512:640]
    for i in range(4):
        sib_u[i].wait_recv()

    def lhs(unit):
        tap, first = unit // 8, pl.ds(pl.multiple_of((unit % 8) * 192, 192), 192)
        return tap, jnp.concatenate(
            [ut[0, 0, first], ut[0, 1 + tap_tile(tap), first],
             ut[1, 0, first], ut[1, 1 + tap_tile(tap), first]], axis=1)

    def tap_tile(tap):
        return tap

    @pl.loop(0, 8)
    def _(g):
        yy, xp = g // 2, g % 2
        parts = []
        for q in range(3):
            tap, left = lhs(3 * g + q)
            parts.append(dot(left, dw[tap, :, 0:256]))
        acc = jnp.concatenate(parts, axis=0)
        pb[2 * xp, yy] = acc[0:288, 0:128].astype(BF)
        pb[2 * xp + 1, yy] = acc[288:576, 0:128].astype(BF)
        for zz in range(4):
            pc[zz, yy, xp] = jnp.concatenate(
                [acc[72 * zz:72 * zz + 72, 128:256], acc[288 + 72 * zz:360 + 72 * zz, 128:256]],
                axis=0).astype(BF)

    ring_start("B")
    ring_start("C")

    @pl.when(c == 0)
    def _():
        @pl.loop(0, 8)
        def _(g):
            yy, xp = g // 2, g % 2
            for q in range(3):
                tap, left = lhs(3 * g + q)
                row = pl.multiple_of(320 + 576 * xp + 192 * q, 64)
                pa[yy, pl.ds(row, 192)] = dot(left, dw[tap, :, 256:384]).astype(BF)

        ring_start("A")

    @pl.when(has_prev)
    def _():
        dz_up.wait_recv()

    @pl.when(jnp.logical_not(has_prev))
    def _():
        dzx[0:D] = jnp.zeros((D, H), BF)

    @pl.when(has_next)
    def _():
        dz_dn.wait_recv()

    @pl.when(jnp.logical_not(has_next))
    def _():
        dzx[D + T:D + T + D] = jnp.zeros((D, H), BF)

    def du(lo, hi):
        @pl.loop(lo, hi)
        def _(n):
            cols = pl.ds(pl.multiple_of(256 * n, 256), 256)
            acc = jnp.zeros((T, 256), F32)
            for k in range(3):
                rows = pl.ds(pl.multiple_of(C * k + 256 * n, 256), 256)
                acc += dot_nt(dzx[D * (2 - k):D * (2 - k) + T], fw[rows])
            v = xe[D:D + T, cols].astype(F32)
            ig[:, cols] = (cot[0:T, cols].astype(F32) + acc * slope(v, tanh_of(v))).astype(BF)

    ring_relay("B")
    ring_relay("C")
    ring_relay("A")
    du(0, 3)

    def second(part, axis, q, rq, sem):
        return [remote(q.at[(pos[axis] + d) % 4], rq.at[d - 1], (sem + d - 1, sem + d - 1), at(axis, d, c))
                for d in (1, 2, 3)]

    sec_a = second("A", "x", qa, rqa, S_P2)
    sec_b = second("B", "z", qb, rqb, S_P2 + 3)
    sec_c = second("C", "y", qc, rqc, S_P2 + 6)

    def up32(v):
        return v.astype(F32)

    ring_end("B")
    for h in range(2):
        s = up32(pb[x, pl.ds(2 * h, 2)]) + up32(rfb[0, 1 - h]) + up32(rfb[1, h])
        for zz in range(4):
            qb[zz, pl.ds(144 * h, 144)] = jnp.concatenate(
                [s[0, 72 * zz:72 * zz + 72], s[1, 72 * zz:72 * zz + 72]], axis=0).astype(BF)
    for cp in sec_b:
        cp.start()

    ring_end("C")
    for h in range(2):
        s = up32(pc[z, pl.ds(2 * h, 2)]) + up32(rfc[0, 1 - h]) + up32(rfc[1, h])
        for yy in range(2):
            for xp in range(2):
                qc[2 * h + yy, pl.ds(144 * xp, 144)] = s[yy, xp].astype(BF)
    for cp in sec_c:
        cp.start()

    ring_end("A")
    for h in range(2):
        sa[pl.ds(800 * h, 800)] = (
            up32(pa[y, pl.ds(800 * h, 800)]) + up32(rfa[0, 1 - h]) + up32(rfa[1, h]))

    def pair(p):
        for xx in range(4):
            lo = 320 * p + 40 * xx
            qa[xx, pl.ds(80 * p, 80)] = jnp.concatenate(
                [sa[lo:lo + 40], sa[lo + 160:lo + 200]], axis=0).astype(BF)

    pair(0)

    @pl.when(c == 0)
    def _():
        for xx in range(4):
            qa[xx, 80:368] = sa[320 + 288 * xx:608 + 288 * xx].astype(BF)
            qa[xx, 368:400] = jnp.zeros((32, 128), BF)

    @pl.when(c == 1)
    def _():
        for p in range(1, 5):
            pair(p)

    for cp in sec_a:
        cp.start()

    du(3, 6)
    store_ig = local(ig, ig_hbm.at[0], 6)
    store_ig.start()

    def third(axis, t, rt, sem):
        i = pos[axis]
        out = []
        for d in (1, 2, 3):
            for cc in (0, 1):
                out.append(remote(t.at[(i + d) % 4, cc], rt.at[c, d],
                                  (sem + 4 * cc + d, sem + 4 * c + d), at(axis, d, cc)))
        out.append(remote(t.at[i, o], rt.at[c, 0], (sem + 4 * o, sem + 4 * c), sibling))
        wait = []
        for s in (0, 1):
            for d in (1, 2, 3):
                wait.append(remote(t.at[0, 0], rt.at[s, d], (sem + 4 * s + d, sem + 4 * s + d), sibling))
        wait.append(remote(t.at[0, 0], rt.at[o, 0], (sem + 4 * o, sem + 4 * o), sibling))
        return out, wait

    thr_a = third("z", ta, rta, S_P3)
    thr_b = third("y", tb, rtb, S_P3 + 8)
    thr_c = third("x", tc, rtc, S_P3 + 16)

    def gather(sec, q, rq, mine, s2, rows):
        for cp in sec:
            cp.wait_recv()
        s2[0:rows] = up32(q[mine]) + up32(rq[0]) + up32(rq[1]) + up32(rq[2])

    def rows36(s2, t, i, first, at_row):
        for cc in range(2):
            lo = first + 72 * i + 36 * cc
            t[i, cc, at_row:at_row + 48] = s2[lo:lo + 48].astype(BF)

    s2b[288:304] = jnp.zeros((16, 128), F32)
    s2c[288:304] = jnp.zeros((16, 128), F32)
    s2a[400:408] = jnp.zeros((8, 128), F32)
    for sec, thr, q, rq, mine, s2, t, rt, i in (
            (sec_b, thr_b, qb, rqb, z, s2b, tb, rtb, y), (sec_c, thr_c, qc, rqc, y, s2c, tc, rtc, x)):
        gather(sec, q, rq, mine, s2, 288)
        for n in range(4):
            rows36(s2, t, n, 0, 0)
        for cp in thr[0]:
            cp.start()
        rt[c, 0] = t[i, c]

    gather(sec_a, qa, rqa, x, s2a, 400)

    def fives(p):
        for n in range(4):
            for cc in range(2):
                lo = 80 * p + 10 * n + 5 * cc
                ta[n, cc, pl.ds(16 * p, 16)] = jnp.concatenate(
                    [s2a[lo:lo + 8], s2a[lo + 40:lo + 48]], axis=0).astype(BF)

    fives(0)

    @pl.when(c == 0)
    def _():
        for n in range(4):
            rows36(s2a, ta, n, 80, 16)
            for cc in range(2):
                ta[n, cc, 64:80] = jnp.zeros((16, 128), BF)

    @pl.when(c == 1)
    def _():
        for p in range(1, 5):
            fives(p)

    for cp in thr_a[0]:
        cp.start()
    rta[c, 0] = ta[z, c]

    scale = 1.0 / (4 * 8192) ** 0.5

    def total(rt, s):
        return (up32(rt[s, 0]) + up32(rt[s, 1]) + up32(rt[s, 2]) + up32(rt[s, 3])) * scale

    for cp in thr_b[1]:
        cp.wait_recv()
    for s in range(2):
        fo_ref[:, 256 * s:256 * s + 128] = total(rtb, s)[0:36]
    for cp in thr_c[1]:
        cp.wait_recv()
    for s in range(2):
        fo_ref[:, 256 * s + 128:256 * s + 256] = total(rtc, s)[0:36]
    for cp in thr_a[1]:
        cp.wait_recv()
    low = total(rta, 0)
    fo_ref[:, 512:640] = low[16:52]
    for b in range(2):
        po_ref[:, 128 * b:128 * b + 128] = low[8 * b:8 * b + 5]
    high = total(rta, 1)
    for b in range(10):
        po_ref[:, 128 * (b + 2):128 * (b + 3)] = high[8 * b:8 * b + 5]

    @pl.when(has_next)
    def _():
        halo_up.wait_send()
        dz_up.wait_send()

    @pl.when(has_prev)
    def _():
        halo_dn.wait_send()
        dz_dn.wait_send()

    for cp in [sib_c, sib_g, sib_d] + sib_u:
        cp.wait_send()
    for part in rings:
        for k in (0, 1):
            for w in range(3):
                steps[part][k][w].wait_send()
    for cp in sec_a + sec_b + sec_c + thr_a[0] + thr_b[0] + thr_c[0]:
        cp.wait_send()
    store_ig.wait()


def shards(inputs, cotangent, filter_weight, projection_weight):
    v = pltpu.VMEM
    anywhere = pl.BlockSpec(memory_space=pl.ANY)
    whole = pl.BlockSpec(memory_space=pltpu.VMEM)
    scratch = [
        v((T + 2 * D, C), BF), v((T + 2 * D, C), BF), v((2, 4, C, 128), BF), v((2 * T, C), BF),
        v((3 * C, H), BF), v((H, C), BF), v((T, H), F32), v((T, H), F32), v((T, H), BF),
        v((2, H, T), BF), v((2, T, H), BF), v((T + 2 * D, H), BF), v((3, 2 * T, 384), BF),
        v((4, RA, 128), BF), v((4, 4, 288, 128), BF), v((4, 4, 2, 144, 128), BF),
        v((2, RA // 2, 128), BF), v((2, 2, 288, 128), BF), v((2, 2, 2, 144, 128), BF),
        v((2, 2, RA // 2, 128), BF), v((2, 2, 2, 288, 128), BF), v((2, 2, 2, 2, 144, 128), BF),
        v((RA, 128), F32), v((4, 400, 128), BF), v((4, 288, 128), BF), v((4, 288, 128), BF),
        v((3, 400, 128), BF), v((3, 288, 128), BF), v((3, 288, 128), BF),
        v((408, 128), F32), v((304, 128), F32), v((304, 128), F32),
        v((4, 2, 80, 128), BF), v((4, 2, 48, 128), BF), v((4, 2, 48, 128), BF),
        v((2, 4, 80, 128), BF), v((2, 4, 48, 128), BF), v((2, 4, 48, 128), BF),
        v((T, C), BF),
        pltpu.SemaphoreType.DMA((8,)), pltpu.SemaphoreType.DMA((N_SEM,)), pltpu.SemaphoreType.DMA((N_SEM,)),
    ]
    return pl.pallas_call(
        kernel,
        name="block_backward",
        out_shape=(
            jax.ShapeDtypeStruct((1, T, C), BF),
            jax.ShapeDtypeStruct((36, H), F32),
            jax.ShapeDtypeStruct((5, C), F32),
        ),
        in_specs=[anywhere] * 4,
        out_specs=(anywhere, whole, whole),
        scratch_shapes=scratch,
        compiler_params=pltpu.CompilerParams(
            collective_id=0, has_side_effects=True, vmem_limit_bytes=56 * 2**20),
        cost_estimate=pl.CostEstimate(flops=5_600_000_000, bytes_accessed=12_000_000, transcendentals=1_000_000),
    )(inputs, cotangent, filter_weight, projection_weight)


def solution(mesh):
    in_specs = (P("grp", "seq", None), P("grp", "seq", None), P(), P())
    out_specs = (P("grp", "seq", None), P(("seq", "grp"), None), P(("seq", "grp"), None))
    return jax.shard_map(shards, mesh=mesh, in_specs=in_specs, out_specs=out_specs, check_vma=False)
```

time: 619 us -> 60.5 us (0.10)
  blocking collectives: 361 us -> 0 us
  starting transfers between devices: 117 us -> 0 us
  Pallas kernels: 0 us -> 54.6 us
  local copies, waits for them, and re-layouts: 55.9 us -> 5.03 us
  waiting for transfers between devices: 38.8 us -> 0 us
  matrix products: 26.6 us -> 0 us
  between operations: 14.7 us -> 0.64 us
    unnamed x1 -> x0, blocking collectives: 361 us -> none
    unnamed x33 -> x0, starting transfers between devices: 106 us -> none
    pallas_call x0 -> x1, Pallas kernels: none -> 54.6 us  [shards(): pl.pallas_call(kernel, name='block_backward', out_shape=(jax.ShapeDtypeSt...]
    unnamed x46 -> x3, local copies, waits for them, and re-layouts: 55.9 us -> 5.03 us
    unnamed x34 -> x0, waiting for transfers between devices: 28.4 us -> none
    dot_general x7 -> x0, matrix products: 26.6 us -> none  [the longest x3 8.86 us: shards(): lax.dot_general(pieces[k], filter_weight[k * chans:(k + 1) * chans], (((1...]
    ppermute x4 -> x0, starting transfers between devices: 11 us -> none  [the longest x2 8.27 us: with_halo(): lax.ppermute(lax.slice_in_dim(block, block.shape[dim] - width, None, axis...]
    ppermute x4 -> x0, waiting for transfers between devices: 10.4 us -> none  [the longest x2 8.33 us: with_halo(): lax.ppermute(lax.slice_in_dim(block, 0, width, axis=dim), axis, backward)]
  transfers between devices with their start and end apart: 37 -> 0, of which waited for: 4 -> 0; matrix products, arithmetic and copies ran while one was open for 10% -> 0% of each run, Pallas kernels for 0% -> 0%
where the time goes in v1:
time: 60.5 us; the launch traced here: 60.2 us
  Pallas kernels  54.6 us (90%)
  local copies, waits for them, and re-layouts  5.03 us (8%)
  between operations  0.64 us (1%)
    pallas_call x1, Pallas kernels, shards(): pl.pallas_call(kernel, name='block_backward', out_shape=(jax.ShapeDtypeSt...  54.6 us
    unnamed x3, local copies, waits for them, and re-layouts  5.03 us

profile of v1, /device:TPU:1, one launch (start us, length us, event | category | flops | bytes accessed | tf_op | source)
XLA Modules:
  0.0 60.2 jit_solution(14080358427498541175)
XLA Ops:
  0.6 54.6 %block_backward.1 = (bf16[1,256,1536]{2,1,0:T(8,128)(2,1)}, f32[36,640]{1,0:T(8,128)}, f32[5,1536]{1,0:T(8,128)}) custom-call(bf16[1,256,1536]{2,1,0:T(8,128)(2,1)} %x_hbm.1, bf16[1,256,1536]{2,1,0:T(8,128)(2,1)} %cot_hbm.1, bf16[4608,640]{1,0:T(8,128)(2,1)} %fw_hbm.1, bf16[640,1536]{1,0:T(8,128)(2,1)} %pw_hbm.1), custom_call_target="tpu_custom_call" | custom-call | flops 5600000000 | bytes 12000000 | tf_op jit(solution)/shard_map/block_backward/pallas_call | solution.py:530
  55.2 2.1 %copy.10 = bf16[1,256,1536]{2,1,0:T(8,128)(2,1)} copy(bf16[1,256,1536]{2,1,0:T(8,128)(2,1)} %get-tuple-element.6) | data formatting | bytes 1572864
  57.3 1.5 %copy.11 = f32[36,640]{1,0:T(8,128)} copy(f32[36,640]{1,0:T(8,128)} %get-tuple-element.7) | data formatting | bytes 184320
  58.8 1.4 %copy.12 = f32[5,1536]{1,0:T(8,128)} copy(f32[5,1536]{1,0:T(8,128)} %get-tuple-element.8) | data formatting | bytes 61440

commit v2 on v1

v2 whole, which is shorter than its diff:
```python
import jax
import jax.numpy as jnp
from jax import lax
from jax.experimental import pallas as pl
from jax.experimental.pallas import tpu as pltpu
from jax.sharding import PartitionSpec as P

MESH = pl.DeviceIdType.MESH
BF, F32 = jnp.bfloat16, jnp.float32
D = 64
T = 256
C = 1536
H = 640
COEFF = 0.7978845608028654
NT = (((1,), (1,)), ((), ()))

S_HALO = 0
S_DZ = 2
S_SIB = 4
S_P1 = 10
S_P2 = 34
S_P3 = 46
N_SEM = 78


def tanh_of(v):
    return jnp.tanh(COEFF * (v + 0.044715 * (v * v * v)))


def slope(v, t):
    return 0.5 * (1.0 + t) + 0.5 * v * (1.0 - t * t) * COEFF * (1.0 + 3.0 * 0.044715 * v * v)


def dot(a, b):
    return jnp.dot(a, b, preferred_element_type=F32)


def dot_nt(a, b):
    return lax.dot_general(a, b, NT, preferred_element_type=F32)


def up32(v):
    return v.astype(F32)


def kernel(x_hbm, cot_hbm, fw_hbm, pw_hbm, ig_hbm, fo_ref, po_ref,
           xv, ue, ut, cot, fw, pw, eo, ei, z_ref, dg_ref, g_ref, gt, dzx, dzc,
           pa, pf, pb, pc, rla, rlf, rlb, rlc, rfa, rff, rfb, rfc,
           sa, sf, qa, qf, qb, qc, rqa, rqf, rqb, rqc, s2a, s2f, s2b, s2c,
           ta, tf, tb, tc, rta, rtf, rtb, rtc, ig, lsem, ssem, rsem):
    seq, grp = lax.axis_index("seq"), lax.axis_index("grp")
    y, x, z, c = seq // 8, (seq // 2) % 4, (seq % 2) * 2 + grp // 2, grp % 2
    o = 1 - c

    def dev(xx, yy, zz, cc):
        return (yy * 8 + xx * 2 + zz // 2, (zz % 2) * 2 + cc)

    def at(axis, d, cc):
        xx = (x + d) % 4 if axis == "x" else x
        yy = (y + d) % 4 if axis == "y" else y
        zz = (z + d) % 4 if axis == "z" else z
        return dev(xx, yy, zz, cc)

    sibling = (seq, grp + 1 - 2 * c)
    pos = {"x": x, "y": y, "z": z}
    has_prev, has_next = seq > 0, seq < 31
    nxt, prv = (seq + 1, grp), (seq - 1, grp)

    def remote(src, dst, sem, device):
        return pltpu.make_async_remote_copy(
            src_ref=src, dst_ref=dst, send_sem=ssem.at[sem[0]], recv_sem=rsem.at[sem[1]],
            device_id=device, device_id_type=MESH)

    def local(src, dst, i):
        return pltpu.make_async_copy(src, dst, lsem.at[i])

    load_x = local(x_hbm.at[0], xv, 0)
    load_f = [local(fw_hbm.at[pl.ds(C * k, C)], fw.at[pl.ds(C * k, C)], 1 + k) for k in range(3)]
    load_c = local(cot_hbm.at[0], cot.at[pl.ds(0, T)], 4)
    load_p = local(pw_hbm, pw, 5)
    load_x.start()
    load_f[0].start()
    load_f[2].start()

    barrier = pltpu.get_barrier_semaphore()

    def greet(device):
        pl.semaphore_signal(barrier, inc=1, device_id=device, device_id_type=MESH)

    @pl.when(has_next)
    def _():
        greet(nxt)

    @pl.when(has_prev)
    def _():
        greet(prv)

    greet(sibling)
    for axis in ("x", "y", "z"):
        for d in (1, 2, 3):
            for cc in (0, 1):
                greet(at(axis, d, cc))

    def act(first, rows):
        v = up32(xv[pl.ds(first, rows)])
        ue[pl.ds(first, rows)] = (0.5 * v * (1.0 + tanh_of(v))).astype(BF)

    load_x.wait()
    for first in (192, 224, 0, 32):
        act(first, 32)
    load_f[0].wait()
    eo[0] = dot(ue[T - D:T], fw[0:C]).astype(BF)
    load_f[2].wait()
    load_f[1].start()
    load_c.start()
    load_p.start()
    eo[1] = dot(ue[0:D], fw[2 * C:3 * C]).astype(BF)

    pl.semaphore_wait(barrier, 19 + has_prev.astype(jnp.int32) + has_next.astype(jnp.int32))

    halo_up = remote(eo.at[0], ei.at[0], (S_HALO, S_HALO), nxt)
    halo_dn = remote(eo.at[1], ei.at[1], (S_HALO + 1, S_HALO + 1), prv)
    dz_up = remote(dzx.at[0, pl.ds(T, D)], dzx.at[0, pl.ds(0, D)], (S_DZ, S_DZ), nxt)
    dz_dn = remote(dzx.at[0, pl.ds(D, D)], dzx.at[0, pl.ds(D + T, D)], (S_DZ + 1, S_DZ + 1), prv)

    @pl.when(has_next)
    def _():
        halo_up.start()

    @pl.when(has_prev)
    def _():
        halo_dn.start()

    sib_c = remote(cot_hbm.at[0], cot.at[pl.ds(T, T)], (S_SIB, S_SIB), sibling)
    sib_u = remote(ut.at[0], ut.at[1], (S_SIB + 1, S_SIB + 1), sibling)
    sib_g = remote(gt.at[0], gt.at[1], (S_SIB + 2, S_SIB + 2), sibling)

    def sib_dz(first, rows, sem):
        return remote(dzx.at[0, pl.ds(first, rows)], dzx.at[1, pl.ds(first, rows)], (sem, sem), sibling)

    sib_d = sib_dz(D, T, S_SIB + 3)
    sib_lo = sib_dz(0, D, S_SIB + 4)
    sib_hi = sib_dz(D + T, D, S_SIB + 5)
    sib_c.start()

    @pl.loop(0, 4)
    def _(i):
        act(pl.multiple_of(D + i * 32, 32), 32)

    ut[0, :, 0:128] = ue[0:128].T
    ut[0, :, 128:256] = ue[128:256].T
    sib_u.start()

    load_f[1].wait()
    z_ref[...] = dot(ue[...], fw[C:2 * C])
    z_ref[64:256] += dot(ue[0:192], fw[0:C])
    z_ref[0:192] += dot(ue[64:256], fw[2 * C:3 * C])
    load_c.wait()
    load_p.wait()
    dg_ref[...] = dot_nt(cot[0:T], pw[...])

    def inner(first):
        rows = pl.ds(first, 32)
        v = z_ref[rows]
        t = tanh_of(v)
        g_ref[rows] = (0.5 * v * (1.0 + t)).astype(BF)
        dzx[0, pl.ds(D + first, 32)] = (dg_ref[rows] * slope(v, t)).astype(BF)

    for first in (64, 96, 128, 160):
        inner(first)

    @pl.when(has_prev)
    def _():
        halo_up.wait_recv()
        z_ref[0:64] += up32(ei[0])

    @pl.when(has_next)
    def _():
        halo_dn.wait_recv()
        z_ref[192:256] += up32(ei[1])

    for first in (0, 32, 192, 224):
        inner(first)

    @pl.when(has_next)
    def _():
        dz_up.start()

    @pl.when(has_prev)
    def _():
        dz_dn.start()

    gt[0] = g_ref[...].T
    sib_g.start()
    sib_d.start()

    rings = {
        "A": ("y", lambda j, h: pa.at[j, pl.ds(320 * h, 320)], rla, rfa, S_P1),
        "F": ("y", lambda j, h: pf.at[j, pl.ds(576 * h, 576)], rlf, rff, S_P1 + 6),
        "G": ("y", lambda j, h: pf.at[j, pl.ds(320 * h, 320)], rlf.at[:, 0:320], rff.at[:, :, 0:320], S_P1 + 6),
        "B": ("x", lambda j, h: pb.at[j, pl.ds(2 * h, 2)], rlb, rfb, S_P1 + 12),
        "C": ("z", lambda j, h: pc.at[j, pl.ds(2 * h, 2)], rlc, rfc, S_P1 + 18),
    }

    def ring(part):
        axis, chunk, rl, rf, sem = rings[part]
        i = pos[axis]
        up, far, dn = (i + 1) % 4, (i + 2) % 4, (i + 3) % 4
        out = []
        for k, (near, h, to) in enumerate(((up, 0, 1), (dn, 1, 3))):
            who = at(axis, to, c)
            s = sem + 3 * k
            out.append((
                remote(chunk(far, h), rl.at[k], (s, s), who),
                remote(chunk(near, 1 - h), rf.at[k, 0], (s + 1, s + 1), who),
                remote(chunk(near, h), rf.at[k, 1], (s + 2, s + 2), who),
                chunk(near, h), rl.at[k]))
        return out

    steps = {part: ring(part) for part in rings}

    def ring_start(part):
        for which in (0, 1):
            for k in (0, 1):
                steps[part][k][which].start()

    def ring_relay(part):
        for k in (0, 1):
            first, _, second, mine, came = steps[part][k]
            first.wait_recv()
            mine[...] = (up32(mine[...]) + up32(came[...])).astype(BF)
            second.start()

    def ring_end(part):
        for k in (0, 1):
            steps[part][k][1].wait_recv()
            steps[part][k][2].wait_recv()

    def proj(to, first, n):
        cols = pl.ds(pl.multiple_of(first, 256), 256)
        acc = dot(gt[0], cot[0:T, cols]) + dot(gt[1], cot[T:2 * T, cols])
        for j in range(4):
            for b in range(2):
                to[j, 320 * n + 160 * b:320 * n + 160 * (b + 1)] = (
                    acc[160 * j:160 * (j + 1), 128 * b:128 * (b + 1)].astype(BF))

    sib_c.wait_recv()
    sib_g.wait_recv()
    for n in range(2):
        proj(pa, 512 * c + 256 * n, n)
    ring_start("A")

    @pl.when(c == 1)
    def _():
        for n in range(2):
            proj(pf, 1024 + 256 * n, n)
        ring_start("G")

    def columns(s, first, rows):
        r = pl.ds(first, rows)
        dzc[s, r, 0:256] = dzx[s, r, pl.ds(pl.multiple_of(256 * c, 256), 256)]
        dzc[s, r, 256:384] = dzx[s, r, 512:640]

    def rhs(tap, lo, hi):
        r = pl.ds(D * (2 - tap), T)
        return jnp.concatenate([dzc[0, r, lo:hi], dzc[1, r, lo:hi]], axis=0)

    def rows_of(first, rows, lo, hi):
        out = []
        last = first + rows
        while first < last:
            tap = first // C
            stop = min(last, C * (tap + 1))
            r = slice(first - C * tap, stop - C * tap)
            left = jnp.concatenate([ut[0, r], ut[1, r]], axis=1)
            out.append(dot(left, rhs(tap, lo, hi)))
            first = stop
        return out[0] if len(out) == 1 else jnp.concatenate(out, axis=0)

    def filt(n):
        yy, xp = n // 2, n % 2
        acc = rows_of(576 * n, 576, 0, 256)
        pb[2 * xp, yy] = acc[0:288, 0:128].astype(BF)
        pb[2 * xp + 1, yy] = acc[288:576, 0:128].astype(BF)
        for zz in range(4):
            pc[zz, yy, xp] = jnp.concatenate(
                [acc[72 * zz:72 * zz + 72, 128:256], acc[288 + 72 * zz:360 + 72 * zz, 128:256]],
                axis=0).astype(BF)

    columns(0, D, T)
    sib_u.wait_recv()
    sib_d.wait_recv()
    columns(1, D, T)
    filt(3)
    filt(4)
    @pl.when(has_prev)
    def _():
        dz_up.wait_recv()

    @pl.when(jnp.logical_not(has_prev))
    def _():
        dzx[0, 0:D] = jnp.zeros((D, H), BF)

    sib_lo.start()

    @pl.when(has_next)
    def _():
        dz_dn.wait_recv()

    @pl.when(jnp.logical_not(has_next))
    def _():
        dzx[0, D + T:D + T + D] = jnp.zeros((D, H), BF)

    sib_hi.start()
    columns(0, 0, D)
    columns(0, D + T, D)
    ring_relay("A")
    sib_lo.wait_recv()
    sib_hi.wait_recv()
    columns(1, 0, D)
    columns(1, D + T, D)
    for n in (0, 1, 2, 5, 6, 7):
        filt(n)
    ring_start("B")
    ring_start("C")

    @pl.when(c == 0)
    def _():
        for n in range(8):
            pf[n // 2, 576 * (n % 2):576 * (n % 2 + 1)] = rows_of(576 * n, 576, 256, 384).astype(BF)
        ring_start("F")

    def du(lo, hi):
        @pl.loop(lo, hi)
        def _(n):
            cols = pl.ds(pl.multiple_of(256 * n, 256), 256)
            acc = jnp.zeros((T, 256), F32)
            for k in range(3):
                rows = pl.ds(pl.multiple_of(C * k + 256 * n, 256), 256)
                acc += dot_nt(dzx[0, D * (2 - k):D * (2 - k) + T], fw[rows])
            v = up32(xv[:, cols])
            ig[:, cols] = (up32(cot[0:T, cols]) + acc * slope(v, tanh_of(v))).astype(BF)

    def second(axis, q, rq, sem):
        return [remote(q.at[(pos[axis] + d) % 4], rq.at[d - 1], (sem + d - 1, sem + d - 1), at(axis, d, c))
                for d in (1, 2, 3)]

    sec_a = second("x", qa, rqa, S_P2)
    sec_f = second("x", qf, rqf, S_P2 + 3)
    sec_b = second("z", qb, rqb, S_P2 + 6)
    sec_c = second("y", qc, rqc, S_P2 + 9)

    def third(axis, t, rt, sem):
        i = pos[axis]
        out = []
        for d in (2, 1, 3):
            for cc in (0, 1):
                out.append(remote(t.at[(i + d) % 4, cc], rt.at[c, d],
                                  (sem + 4 * cc + d, sem + 4 * c + d), at(axis, d, cc)))
        out.append(remote(t.at[i, o], rt.at[c, 0], (sem + 4 * o, sem + 4 * c), sibling))
        wait = []
        for s in (0, 1):
            for d in (1, 2, 3):
                wait.append(remote(t.at[0, 0], rt.at[s, d], (sem + 4 * s + d, sem + 4 * s + d), sibling))
        wait.append(remote(t.at[0, 0], rt.at[o, 0], (sem + 4 * o, sem + 4 * o), sibling))
        return out, wait

    thr_a = third("z", ta, rta, S_P3)
    thr_f = third("z", tf, rtf, S_P3 + 8)
    thr_b = third("y", tb, rtb, S_P3 + 16)
    thr_c = third("x", tc, rtc, S_P3 + 24)

    def begin(copies):
        for cp in copies:
            cp.start()

    def pairs(q, s):
        for p in range(2):
            for xx in range(4):
                lo = 320 * p + 40 * xx
                q[xx, 80 * p:80 * (p + 1)] = jnp.concatenate(
                    [s[lo:lo + 40], s[lo + 160:lo + 200]], axis=0).astype(BF)

    def gather(sec, q, rq, mine, s2, rows):
        for cp in sec:
            cp.wait_recv()
        s2[0:rows] = up32(q[mine]) + up32(rq[0]) + up32(rq[1]) + up32(rq[2])

    def rows36(s2, t):
        for n in range(4):
            for cc in range(2):
                lo = 72 * n + 36 * cc
                t[n, cc] = s2[lo:lo + 48].astype(BF)

    def fives(s2, t):
        for p in range(2):
            for n in range(4):
                for cc in range(2):
                    lo = 80 * p + 10 * n + 5 * cc
                    t[n, cc, 16 * p:16 * (p + 1)] = jnp.concatenate(
                        [s2[lo:lo + 8], s2[lo + 40:lo + 48]], axis=0).astype(BF)

    @pl.when(c == 1)
    def _():
        ring_relay("G")

    du(0, 3)
    ring_relay("B")
    ring_relay("C")

    @pl.when(c == 0)
    def _():
        ring_relay("F")
    ring_end("A")
    for h in range(2):
        sa[320 * h:320 * (h + 1)] = up32(pa[y, 320 * h:320 * (h + 1)]) + up32(rfa[0, 1 - h]) + up32(rfa[1, h])
    pairs(qa, sa)
    begin(sec_a)


    s2a[160:168] = jnp.zeros((8, 128), F32)
    s2f[288:304] = jnp.zeros((16, 128), F32)
    s2b[288:304] = jnp.zeros((16, 128), F32)
    s2c[288:304] = jnp.zeros((16, 128), F32)
    ring_end("B")
    for h in range(2):
        s = up32(pb[x, pl.ds(2 * h, 2)]) + up32(rfb[0, 1 - h]) + up32(rfb[1, h])
        for zz in range(4):
            qb[zz, pl.ds(144 * h, 144)] = jnp.concatenate(
                [s[0, 72 * zz:72 * zz + 72], s[1, 72 * zz:72 * zz + 72]], axis=0).astype(BF)
    begin(sec_b)

    ring_end("C")
    for h in range(2):
        s = up32(pc[z, pl.ds(2 * h, 2)]) + up32(rfc[0, 1 - h]) + up32(rfc[1, h])
        for yy in range(2):
            for xp in range(2):
                qc[2 * h + yy, pl.ds(144 * xp, 144)] = s[yy, xp].astype(BF)
    begin(sec_c)

    def sum_f(rows):
        for h in range(2):
            r = pl.ds(rows * h, rows)
            sf[r] = up32(pf[y, r]) + up32(rff[0, 1 - h, 0:rows]) + up32(rff[1, h, 0:rows])

    @pl.when(c == 0)
    def _():
        ring_end("F")
        sum_f(576)
        for xx in range(4):
            qf[xx] = sf[288 * xx:288 * (xx + 1)].astype(BF)

    @pl.when(c == 1)
    def _():
        ring_end("G")
        sum_f(320)
        pairs(qf, sf)
        for xx in range(4):
            qf[xx, 160:288] = jnp.zeros((128, 128), BF)

    begin(sec_f)
    du(3, 6)
    store_ig = local(ig, ig_hbm.at[0], 6)
    store_ig.start()
    gather(sec_a, qa, rqa, x, s2a, 160)
    fives(s2a, ta)
    begin(thr_a[0])
    rta[c, 0] = ta[z, c]

    for sec, thr, q, rq, mine, s2, t, rt, i in (
            (sec_b, thr_b, qb, rqb, z, s2b, tb, rtb, y), (sec_c, thr_c, qc, rqc, y, s2c, tc, rtc, x)):
        gather(sec, q, rq, mine, s2, 288)
        rows36(s2, t)
        begin(thr[0])
        rt[c, 0] = t[i, c]

    gather(sec_f, qf, rqf, x, s2f, 288)

    @pl.when(c == 0)
    def _():
        rows36(s2f, tf)

    @pl.when(c == 1)
    def _():
        fives(s2f, tf)
        for n in range(4):
            for cc in range(2):
                tf[n, cc, 32:48] = jnp.zeros((16, 128), BF)

    begin(thr_f[0])
    rtf[c, 0] = tf[z, c]

    scale = 1.0 / (4 * 8192) ** 0.5

    def total(thr, rt):
        for cp in thr[1]:
            cp.wait_recv()
        return [(up32(rt[s, 0]) + up32(rt[s, 1]) + up32(rt[s, 2]) + up32(rt[s, 3])) * scale for s in range(2)]

    def put_proj(v, first):
        for b in range(4):
            po_ref[:, 128 * (first + b):128 * (first + b + 1)] = v[8 * b:8 * b + 5]

    low, high = total(thr_a, rta)
    put_proj(low, 0)
    put_proj(high, 4)
    for s, v in enumerate(total(thr_b, rtb)):
        fo_ref[:, 256 * s:256 * s + 128] = v[0:36]
    for s, v in enumerate(total(thr_c, rtc)):
        fo_ref[:, 256 * s + 128:256 * s + 256] = v[0:36]
    low, high = total(thr_f, rtf)
    fo_ref[:, 512:640] = low[0:36]
    put_proj(high, 8)

    @pl.when(has_next)
    def _():
        halo_up.wait_send()
        dz_up.wait_send()

    @pl.when(has_prev)
    def _():
        halo_dn.wait_send()
        dz_dn.wait_send()

    for cp in (sib_c, sib_u, sib_g, sib_d, sib_lo, sib_hi):
        cp.wait_send()
    def ring_left(part):
        for k in (0, 1):
            for w in range(3):
                steps[part][k][w].wait_send()

    ring_left("A")
    ring_left("B")
    ring_left("C")

    @pl.when(c == 0)
    def _():
        ring_left("F")

    @pl.when(c == 1)
    def _():
        ring_left("G")

    for cp in sec_a + sec_f + sec_b + sec_c + thr_a[0] + thr_f[0] + thr_b[0] + thr_c[0]:
        cp.wait_send()
    store_ig.wait()


def finish(*refs):
    ins, outs, held, sem = refs[:3], refs[3:6], refs[6:9], refs[9]
    come = [pltpu.make_async_copy(a, v, sem.at[i]) for i, (a, v) in enumerate(zip(ins, held))]
    go = [pltpu.make_async_copy(v, b, sem.at[3 + i]) for i, (v, b) in enumerate(zip(held, outs))]
    for cp in come:
        cp.start()
    for cp, then in zip(come, go):
        cp.wait()
        then.start()
    for cp in go:
        cp.wait()


def shards(inputs, cotangent, filter_weight, projection_weight):
    v = pltpu.VMEM
    anywhere = pl.BlockSpec(memory_space=pl.ANY)
    whole = pl.BlockSpec(memory_space=pltpu.VMEM)
    scratch = [
        v((T, C), BF), v((T, C), BF), v((2, C, T), BF), v((2 * T, C), BF), v((3 * C, H), BF), v((H, C), BF),
        v((2, D, H), BF), v((2, D, H), BF), v((T, H), F32), v((T, H), F32), v((T, H), BF),
        v((2, H, T), BF), v((2, T + 2 * D, H), BF), v((2, T + 2 * D, 384), BF),
        v((4, 640, 128), BF), v((4, 1152, 128), BF), v((4, 4, 288, 128), BF), v((4, 4, 2, 144, 128), BF),
        v((2, 320, 128), BF), v((2, 576, 128), BF), v((2, 2, 288, 128), BF), v((2, 2, 2, 144, 128), BF),
        v((2, 2, 320, 128), BF), v((2, 2, 576, 128), BF), v((2, 2, 2, 288, 128), BF), v((2, 2, 2, 2, 144, 128), BF),
        v((640, 128), F32), v((1152, 128), F32),
        v((4, 160, 128), BF), v((4, 288, 128), BF), v((4, 288, 128), BF), v((4, 288, 128), BF),
        v((3, 160, 128), BF), v((3, 288, 128), BF), v((3, 288, 128), BF), v((3, 288, 128), BF),
        v((168, 128), F32), v((304, 128), F32), v((304, 128), F32), v((304, 128), F32),
        v((4, 2, 32, 128), BF), v((4, 2, 48, 128), BF), v((4, 2, 48, 128), BF), v((4, 2, 48, 128), BF),
        v((2, 4, 32, 128), BF), v((2, 4, 48, 128), BF), v((2, 4, 48, 128), BF), v((2, 4, 48, 128), BF),
        v((T, C), BF),
        pltpu.SemaphoreType.DMA((8,)), pltpu.SemaphoreType.DMA((N_SEM,)), pltpu.SemaphoreType.DMA((N_SEM,)),
    ]
    shapes = (
        jax.ShapeDtypeStruct((1, T, C), BF),
        jax.ShapeDtypeStruct((36, H), F32),
        jax.ShapeDtypeStruct((5, C), F32),
    )
    results = pl.pallas_call(
        kernel,
        name="block_backward",
        out_shape=shapes,
        in_specs=[anywhere] * 4,
        out_specs=(anywhere, whole, whole),
        scratch_shapes=scratch,
        compiler_params=pltpu.CompilerParams(
            collective_id=0, has_side_effects=True, vmem_limit_bytes=56 * 2**20),
        cost_estimate=pl.CostEstimate(flops=5_600_000_000, bytes_accessed=12_000_000, transcendentals=1_000_000),
    )(inputs, cotangent, filter_weight, projection_weight)
    return pl.pallas_call(
        finish,
        name="hand_out",
        out_shape=shapes,
        in_specs=[anywhere] * 3,
        out_specs=[anywhere] * 3,
        scratch_shapes=[v(s.shape, s.dtype) for s in shapes] + [pltpu.SemaphoreType.DMA((6,))],
    )(*results)


def solution(mesh):
    in_specs = (P("grp", "seq", None), P("grp", "seq", None), P(), P())
    out_specs = (P("grp", "seq", None), P(("seq", "grp"), None), P(("seq", "grp"), None))
    return jax.shard_map(shards, mesh=mesh, in_specs=in_specs, out_specs=out_specs, check_vma=False)
```

time: 60.5 us -> 50.3 us (0.83)
  local copies, waits for them, and re-layouts: 5.03 us -> 0 us
  Pallas kernels: 54.6 us -> 49.6 us
    unnamed x3 -> x0, local copies, waits for them, and re-layouts: 5.03 us -> none
    pallas_call x1 -> x2, Pallas kernels: 54.6 us -> 49.6 us  [the longest x1 47.5 us: shards(): pl.pallas_call(kernel, name='block_backward', out_shape=shapes, in_specs=...]
where the time goes in v2:
time: 50.3 us; the launch traced here: 50.2 us
  Pallas kernels  49.6 us (99%)
  between operations  0.64 us (1%)
    pallas_call x1, Pallas kernels, shards(): pl.pallas_call(kernel, name='block_backward', out_shape=shapes, in_specs=...  47.5 us
    pallas_call x1, Pallas kernels, shards(): pl.pallas_call(finish, name='hand_out', out_shape=shapes, in_specs=[anywh...  2.1 us

profile of v2, /device:TPU:1, one launch (start us, length us, event | category | flops | bytes accessed | tf_op | source)
XLA Modules:
  0.0 50.2 jit_solution(11801112508529865050)
XLA Ops:
  0.6 47.5 %block_backward.1 = (bf16[1,256,1536]{2,1,0:T(8,128)(2,1)}, f32[36,640]{1,0:T(8,128)}, f32[5,1536]{1,0:T(8,128)}) custom-call(bf16[1,256,1536]{2,1,0:T(8,128)(2,1)} %x_hbm.1, bf16[1,256,1536]{2,1,0:T(8,128)(2,1)} %cot_hbm.1, bf16[4608,640]{1,0:T(8,128)(2,1)} %fw_hbm.1, bf16[640,1536]{1,0:T(8,128)(2,1)} %pw_hbm.1), custom_call_target="tpu_custom_call" | custom-call | flops 5600000000 | bytes 12000000 | tf_op jit(solution)/shard_map/block_backward/pallas_call | solution.py:587
  48.1 2.1 %hand_out.1 = (bf16[1,256,1536]{2,1,0:T(8,128)(2,1)}, f32[36,640]{1,0:T(8,128)}, f32[5,1536]{1,0:T(8,128)}) custom-call(bf16[1,256,1536]{2,1,0:T(8,128)(2,1)} %get-tuple-element.6.refs_0_, f32[36,640]{1,0:T(8,128)} %get-tuple-element.7.refs_1_, f32[5,1536]{1,0:T(8,128)} %get-tuple-element.8.refs_2_), custom_call_target="tpu_custom_call" | custom-call | tf_op jit(solution)/shard_map/hand_out/pallas_call | solution.py:598

commit v3 on v2

--- a/solution.py
+++ b/solution.py
@@ -18,9 +18,19 @@
 S_DZ = 2
 S_SIB = 4
 S_P1 = 10
-S_P2 = 34
-S_P3 = 46
-N_SEM = 78
+S_P2 = 46
+S_P3 = 58
+N_SEM = 90
+
+
+def slot_b(xx, yy):
+    if yy == (2 if xx < 2 else 1):
+        return 0
+    return {0: 1, 1: 2, 2: 2, 3: 3}[yy]
+
+
+def row_c(yy, xp):
+    return 144 * ((1, 1), (2, 0), (0, 0), (0, 1), (1, 0), (2, 1), (3, 0), (3, 1)).index((yy, xp))
 
 
 def tanh_of(v):
@@ -46,7 +56,7 @@
 def kernel(x_hbm, cot_hbm, fw_hbm, pw_hbm, ig_hbm, fo_ref, po_ref,
            xv, ue, ut, cot, fw, pw, eo, ei, z_ref, dg_ref, g_ref, gt, dzx, dzc,
            pa, pf, pb, pc, rla, rlf, rlb, rlc, rfa, rff, rfb, rfc,
-           sa, sf, qa, qf, qb, qc, rqa, rqf, rqb, rqc, s2a, s2f, s2b, s2c,
+           sa, sf, sb, sc, qa, qf, qb, qc, rqa, rqf, rqb, rqc, s2a, s2f, s2b, s2c,
            ta, tf, tb, tc, rta, rtf, rtb, rtc, ig, lsem, ssem, rsem):
     seq, grp = lax.axis_index("seq"), lax.axis_index("grp")
     y, x, z, c = seq // 8, (seq // 2) % 4, (seq % 2) * 2 + grp // 2, grp % 2
@@ -194,12 +204,20 @@
     sib_g.start()
     sib_d.start()
 
+    def flat(p, first, rows):
+        return lambda j, h: p.at[j, pl.ds(first + rows * h, rows)]
+
+    def cut(r, first, rows):
+        return r.at[..., pl.ds(first, rows), :]
+
     rings = {
-        "A": ("y", lambda j, h: pa.at[j, pl.ds(320 * h, 320)], rla, rfa, S_P1),
-        "F": ("y", lambda j, h: pf.at[j, pl.ds(576 * h, 576)], rlf, rff, S_P1 + 6),
-        "G": ("y", lambda j, h: pf.at[j, pl.ds(320 * h, 320)], rlf.at[:, 0:320], rff.at[:, :, 0:320], S_P1 + 6),
-        "B": ("x", lambda j, h: pb.at[j, pl.ds(2 * h, 2)], rlb, rfb, S_P1 + 12),
-        "C": ("z", lambda j, h: pc.at[j, pl.ds(2 * h, 2)], rlc, rfc, S_P1 + 18),
+        "A": ("y", flat(pa, 0, 320), rla, rfa, S_P1),
+        "F": ("y", flat(pf, 0, 576), rlf, rff, S_P1 + 6),
+        "G": ("y", flat(pf, 0, 320), cut(rlf, 0, 320), cut(rff, 0, 320), S_P1 + 6),
+        "B0": ("x", flat(pb, 0, 144), cut(rlb, 0, 144), cut(rfb, 0, 144), S_P1 + 12),
+        "B1": ("x", flat(pb, 288, 432), cut(rlb, 144, 432), cut(rfb, 144, 432), S_P1 + 18),
+        "C0": ("z", flat(pc, 0, 144), cut(rlc, 0, 144), cut(rfc, 0, 144), S_P1 + 24),
+        "C1": ("z", flat(pc, 288, 432), cut(rlc, 144, 432), cut(rfc, 144, 432), S_P1 + 30),
     }
 
     def ring(part):
@@ -280,10 +298,12 @@
     def filt(n):
         yy, xp = n // 2, n % 2
         acc = rows_of(576 * n, 576, 0, 256)
-        pb[2 * xp, yy] = acc[0:288, 0:128].astype(BF)
-        pb[2 * xp + 1, yy] = acc[288:576, 0:128].astype(BF)
+        for b in range(2):
+            first = 288 * slot_b(2 * xp + b, yy)
+            pb[2 * xp + b, first:first + 288] = acc[288 * b:288 * (b + 1), 0:128].astype(BF)
+        first = row_c(yy, xp)
         for zz in range(4):
-            pc[zz, yy, xp] = jnp.concatenate(
+            pc[zz, first:first + 144] = jnp.concatenate(
                 [acc[72 * zz:72 * zz + 72, 128:256], acc[288 + 72 * zz:360 + 72 * zz, 128:256]],
                 axis=0).astype(BF)
 
@@ -293,6 +313,7 @@
     columns(1, D, T)
     filt(3)
     filt(4)
+    ring_start("B0")
     @pl.when(has_prev)
     def _():
         dz_up.wait_recv()
@@ -314,15 +335,18 @@
     sib_hi.start()
     columns(0, 0, D)
     columns(0, D + T, D)
+    ring_start("C0")
     ring_relay("A")
+    ring_relay("B0")
     sib_lo.wait_recv()
     sib_hi.wait_recv()
     columns(1, 0, D)
     columns(1, D + T, D)
     for n in (0, 1, 2, 5, 6, 7):
         filt(n)
-    ring_start("B")
-    ring_start("C")
+    ring_start("B1")
+    ring_start("C1")
+    ring_relay("C0")
 
     @pl.when(c == 0)
     def _():
@@ -347,6 +371,8 @@
 
     sec_a = second("x", qa, rqa, S_P2)
     sec_f = second("x", qf, rqf, S_P2 + 3)
+    sec_g = [remote(qf.at[(x + d) % 4, pl.ds(0, 160)], rqf.at[d - 1, pl.ds(0, 160)],
+                    (S_P2 + 2 + d, S_P2 + 2 + d), at("x", d, c)) for d in (1, 2, 3)]
     sec_b = second("z", qb, rqb, S_P2 + 6)
     sec_c = second("y", qc, rqc, S_P2 + 9)
 
@@ -384,13 +410,14 @@
     def gather(sec, q, rq, mine, s2, rows):
         for cp in sec:
             cp.wait_recv()
-        s2[0:rows] = up32(q[mine]) + up32(rq[0]) + up32(rq[1]) + up32(rq[2])
-
-    def rows36(s2, t):
-        for n in range(4):
+        r = pl.ds(0, rows)
+        s2[r] = up32(q[mine, r]) + up32(rq[0, r]) + up32(rq[1, r]) + up32(rq[2, r])
+
+    def rows36(s2, t, owners=(0, 1, 2, 3)):
+        for n, owner in enumerate(owners):
             for cc in range(2):
                 lo = 72 * n + 36 * cc
-                t[n, cc] = s2[lo:lo + 48].astype(BF)
+                t[owner, cc] = s2[lo:lo + 48].astype(BF)
 
     def fives(s2, t):
         for p in range(2):
@@ -405,8 +432,8 @@
         ring_relay("G")
 
     du(0, 3)
-    ring_relay("B")
-    ring_relay("C")
+    ring_relay("B1")
+    ring_relay("C1")
 
     @pl.when(c == 0)
     def _():
@@ -422,20 +449,29 @@
     s2f[288:304] = jnp.zeros((16, 128), F32)
     s2b[288:304] = jnp.zeros((16, 128), F32)
     s2c[288:304] = jnp.zeros((16, 128), F32)
-    ring_end("B")
+    def sum_bc(p, i, rf, to):
+        for first, off, rows in ((0, 0, 144), (288, 144, 432)):
+            for h in range(2):
+                r, f = pl.ds(first + rows * h, rows), pl.ds(off, rows)
+                to[r] = up32(p[i, r]) + up32(rf[0, 1 - h, f]) + up32(rf[1, h, f])
+
+    ring_end("B0")
+    ring_end("B1")
+    sum_bc(pb, x, rfb, sb)
     for h in range(2):
-        s = up32(pb[x, pl.ds(2 * h, 2)]) + up32(rfb[0, 1 - h]) + up32(rfb[1, h])
         for zz in range(4):
-            qb[zz, pl.ds(144 * h, 144)] = jnp.concatenate(
-                [s[0, 72 * zz:72 * zz + 72], s[1, 72 * zz:72 * zz + 72]], axis=0).astype(BF)
+            lo = 576 * h + 72 * zz
+            qb[zz, 144 * h:144 * (h + 1)] = jnp.concatenate(
+                [sb[lo:lo + 72], sb[lo + 288:lo + 360]], axis=0).astype(BF)
     begin(sec_b)
 
-    ring_end("C")
-    for h in range(2):
-        s = up32(pc[z, pl.ds(2 * h, 2)]) + up32(rfc[0, 1 - h]) + up32(rfc[1, h])
-        for yy in range(2):
-            for xp in range(2):
-                qc[2 * h + yy, pl.ds(144 * xp, 144)] = s[yy, xp].astype(BF)
+    ring_end("C0")
+    ring_end("C1")
+    sum_bc(pc, z, rfc, sc)
+    for yy in range(4):
+        for xp in range(2):
+            lo = row_c(yy, xp)
+            qc[yy, 144 * xp:144 * (xp + 1)] = sc[lo:lo + 144].astype(BF)
     begin(sec_c)
 
     def sum_f(rows):
@@ -449,16 +485,15 @@
         sum_f(576)
         for xx in range(4):
             qf[xx] = sf[288 * xx:288 * (xx + 1)].astype(BF)
+        begin(sec_f)
 
     @pl.when(c == 1)
     def _():
         ring_end("G")
         sum_f(320)
         pairs(qf, sf)
-        for xx in range(4):
-            qf[xx, 160:288] = jnp.zeros((128, 128), BF)
-
-    begin(sec_f)
+        begin(sec_g)
+
     du(3, 6)
     store_ig = local(ig, ig_hbm.at[0], 6)
     store_ig.start()
@@ -467,21 +502,24 @@
     begin(thr_a[0])
     rta[c, 0] = ta[z, c]
 
-    for sec, thr, q, rq, mine, s2, t, rt, i in (
-            (sec_b, thr_b, qb, rqb, z, s2b, tb, rtb, y), (sec_c, thr_c, qc, rqc, y, s2c, tc, rtc, x)):
+    mid = jnp.where(x < 2, 1, 0)
+    for sec, thr, q, rq, mine, s2, t, rt, i, owners in (
+            (sec_b, thr_b, qb, rqb, z, s2b, tb, rtb, y, (1 + mid, 0, 2 - mid, 3)),
+            (sec_c, thr_c, qc, rqc, y, s2c, tc, rtc, x, (0, 1, 2, 3))):
         gather(sec, q, rq, mine, s2, 288)
-        rows36(s2, t)
+        rows36(s2, t, owners)
         begin(thr[0])
         rt[c, 0] = t[i, c]
 
-    gather(sec_f, qf, rqf, x, s2f, 288)
-
     @pl.when(c == 0)
     def _():
+        gather(sec_f, qf, rqf, x, s2f, 288)
         rows36(s2f, tf)
 
     @pl.when(c == 1)
     def _():
+        gather(sec_g, qf, rqf, x, s2f, 160)
+        s2f[160:168] = jnp.zeros((8, 128), F32)
         fives(s2f, tf)
         for n in range(4):
             for cc in range(2):
@@ -530,18 +568,24 @@
                 steps[part][k][w].wait_send()
 
     ring_left("A")
-    ring_left("B")
-    ring_left("C")
+    ring_left("B0")
+    ring_left("B1")
+    ring_left("C0")
+    ring_left("C1")
 
     @pl.when(c == 0)
     def _():
         ring_left("F")
+        for cp in sec_f:
+            cp.wait_send()
 
     @pl.when(c == 1)
     def _():
         ring_left("G")
-
-    for cp in sec_a + sec_f + sec_b + sec_c + thr_a[0] + thr_f[0] + thr_b[0] + thr_c[0]:
+        for cp in sec_g:
+            cp.wait_send()
+
+    for cp in sec_a + sec_b + sec_c + thr_a[0] + thr_f[0] + thr_b[0] + thr_c[0]:
         cp.wait_send()
     store_ig.wait()
 
@@ -567,10 +611,10 @@
         v((T, C), BF), v((T, C), BF), v((2, C, T), BF), v((2 * T, C), BF), v((3 * C, H), BF), v((H, C), BF),
         v((2, D, H), BF), v((2, D, H), BF), v((T, H), F32), v((T, H), F32), v((T, H), BF),
         v((2, H, T), BF), v((2, T + 2 * D, H), BF), v((2, T + 2 * D, 384), BF),
-        v((4, 640, 128), BF), v((4, 1152, 128), BF), v((4, 4, 288, 128), BF), v((4, 4, 2, 144, 128), BF),
-        v((2, 320, 128), BF), v((2, 576, 128), BF), v((2, 2, 288, 128), BF), v((2, 2, 2, 144, 128), BF),
-        v((2, 2, 320, 128), BF), v((2, 2, 576, 128), BF), v((2, 2, 2, 288, 128), BF), v((2, 2, 2, 2, 144, 128), BF),
-        v((640, 128), F32), v((1152, 128), F32),
+        v((4, 640, 128), BF), v((4, 1152, 128), BF), v((4, 1152, 128), BF), v((4, 1152, 128), BF),
+        v((2, 320, 128), BF), v((2, 576, 128), BF), v((2, 576, 128), BF), v((2, 576, 128), BF),
+        v((2, 2, 320, 128), BF), v((2, 2, 576, 128), BF), v((2, 2, 576, 128), BF), v((2, 2, 576, 128), BF),
+        v((640, 128), F32), v((1152, 128), F32), v((1152, 128), F32), v((1152, 128), F32),
         v((4, 160, 128), BF), v((4, 288, 128), BF), v((4, 288, 128), BF), v((4, 288, 128), BF),
         v((3, 160, 128), BF), v((3, 288, 128), BF), v((3, 288, 128), BF), v((3, 288, 128), BF),
         v((168, 128), F32), v((304, 128), F32), v((304, 128), F32), v((304, 128), F32),

time: 50.3 us -> 49.5 us (0.984)
  Pallas kernels: 49.6 us -> 48.7 us
    pallas_call x1, Pallas kernels: 47.5 us -> 46.6 us  [shards(): pl.pallas_call(kernel, name='block_backward', out_shape=shapes, in_specs=...]
where the time goes in v3:
time: 49.5 us; the launch traced here: 49.4 us
  Pallas kernels  48.7 us (98%)
  between operations  0.64 us (1%)
    pallas_call x1, Pallas kernels, shards(): pl.pallas_call(kernel, name='block_backward', out_shape=shapes, in_specs=...  46.6 us
    pallas_call x1, Pallas kernels, shards(): pl.pallas_call(finish, name='hand_out', out_shape=shapes, in_specs=[anywh...  2.1 us

profile of v3, /device:TPU:1, one launch (start us, length us, event | category | flops | bytes accessed | tf_op | source)
XLA Modules:
  0.0 49.4 jit_solution(15817509654181567783)
XLA Ops:
  0.6 46.6 %block_backward.1 = (bf16[1,256,1536]{2,1,0:T(8,128)(2,1)}, f32[36,640]{1,0:T(8,128)}, f32[5,1536]{1,0:T(8,128)}) custom-call(bf16[1,256,1536]{2,1,0:T(8,128)(2,1)} %x_hbm.1, bf16[1,256,1536]{2,1,0:T(8,128)(2,1)} %cot_hbm.1, bf16[4608,640]{1,0:T(8,128)(2,1)} %fw_hbm.1, bf16[640,1536]{1,0:T(8,128)(2,1)} %pw_hbm.1), custom_call_target="tpu_custom_call" | custom-call | flops 5600000000 | bytes 12000000 | tf_op jit(solution)/shard_map/block_backward/pallas_call | solution.py:631
  47.3 2.1 %hand_out.1 = (bf16[1,256,1536]{2,1,0:T(8,128)(2,1)}, f32[36,640]{1,0:T(8,128)}, f32[5,1536]{1,0:T(8,128)}) custom-call(bf16[1,256,1536]{2,1,0:T(8,128)(2,1)} %get-tuple-element.6.refs_0_, f32[36,640]{1,0:T(8,128)} %get-tuple-element.7.refs_1_, f32[5,1536]{1,0:T(8,128)} %get-tuple-element.8.refs_2_), custom_call_target="tpu_custom_call" | custom-call | tf_op jit(solution)/shard_map/hand_out/pallas_call | solution.py:642

commit v4 on v3

--- a/solution.py
+++ b/solution.py
@@ -18,9 +18,13 @@
 S_DZ = 2
 S_SIB = 4
 S_P1 = 10
-S_P2 = 46
-S_P3 = 58
-N_SEM = 90
+S_P2 = 64
+S_P3 = 76
+N_SEM = 108
+
+
+PIECES = ((0, 0, 144), (288, 144, 224), (736, 368, 208))
+PIECES_F = ((0, 0, 288), (576, 288, 288))
 
 
 def slot_b(xx, yy):
@@ -118,24 +122,24 @@
     load_x.wait()
     for first in (192, 224, 0, 32):
         act(first, 32)
+    pl.semaphore_wait(barrier, 19 + has_prev.astype(jnp.int32) + has_next.astype(jnp.int32))
+    halo_up = remote(eo.at[0], ei.at[0], (S_HALO, S_HALO), nxt)
+    halo_dn = remote(eo.at[1], ei.at[1], (S_HALO + 1, S_HALO + 1), prv)
+    dz_up = remote(dzx.at[0, pl.ds(T, D)], dzx.at[0, pl.ds(0, D)], (S_DZ, S_DZ), nxt)
+    dz_dn = remote(dzx.at[0, pl.ds(D, D)], dzx.at[0, pl.ds(D + T, D)], (S_DZ + 1, S_DZ + 1), prv)
+
     load_f[0].wait()
     eo[0] = dot(ue[T - D:T], fw[0:C]).astype(BF)
+
+    @pl.when(has_next)
+    def _():
+        halo_up.start()
+
     load_f[2].wait()
     load_f[1].start()
     load_c.start()
     load_p.start()
     eo[1] = dot(ue[0:D], fw[2 * C:3 * C]).astype(BF)
-
-    pl.semaphore_wait(barrier, 19 + has_prev.astype(jnp.int32) + has_next.astype(jnp.int32))
-
-    halo_up = remote(eo.at[0], ei.at[0], (S_HALO, S_HALO), nxt)
-    halo_dn = remote(eo.at[1], ei.at[1], (S_HALO + 1, S_HALO + 1), prv)
-    dz_up = remote(dzx.at[0, pl.ds(T, D)], dzx.at[0, pl.ds(0, D)], (S_DZ, S_DZ), nxt)
-    dz_dn = remote(dzx.at[0, pl.ds(D, D)], dzx.at[0, pl.ds(D + T, D)], (S_DZ + 1, S_DZ + 1), prv)
-
-    @pl.when(has_next)
-    def _():
-        halo_up.start()
 
     @pl.when(has_prev)
     def _():
@@ -184,21 +188,24 @@
         halo_up.wait_recv()
         z_ref[0:64] += up32(ei[0])
 
+    inner(0)
+    inner(32)
+
+    @pl.when(has_prev)
+    def _():
+        dz_dn.start()
+
     @pl.when(has_next)
     def _():
         halo_dn.wait_recv()
         z_ref[192:256] += up32(ei[1])
 
-    for first in (0, 32, 192, 224):
-        inner(first)
+    inner(192)
+    inner(224)
 
     @pl.when(has_next)
     def _():
         dz_up.start()
-
-    @pl.when(has_prev)
-    def _():
-        dz_dn.start()
 
     gt[0] = g_ref[...].T
     sib_g.start()
@@ -212,13 +219,13 @@
 
     rings = {
         "A": ("y", flat(pa, 0, 320), rla, rfa, S_P1),
-        "F": ("y", flat(pf, 0, 576), rlf, rff, S_P1 + 6),
         "G": ("y", flat(pf, 0, 320), cut(rlf, 0, 320), cut(rff, 0, 320), S_P1 + 6),
-        "B0": ("x", flat(pb, 0, 144), cut(rlb, 0, 144), cut(rfb, 0, 144), S_P1 + 12),
-        "B1": ("x", flat(pb, 288, 432), cut(rlb, 144, 432), cut(rfb, 144, 432), S_P1 + 18),
-        "C0": ("z", flat(pc, 0, 144), cut(rlc, 0, 144), cut(rfc, 0, 144), S_P1 + 24),
-        "C1": ("z", flat(pc, 288, 432), cut(rlc, 144, 432), cut(rfc, 144, 432), S_P1 + 30),
     }
+    for n, (first, off, rows) in enumerate(PIECES_F):
+        rings[f"F{n}"] = ("y", flat(pf, first, rows), cut(rlf, off, rows), cut(rff, off, rows), S_P1 + 6 + 6 * n)
+    for n, (first, off, rows) in enumerate(PIECES):
+        rings[f"B{n}"] = ("x", flat(pb, first, rows), cut(rlb, off, rows), cut(rfb, off, rows), S_P1 + 18 + 6 * n)
+        rings[f"C{n}"] = ("z", flat(pc, first, rows), cut(rlc, off, rows), cut(rfc, off, rows), S_P1 + 36 + 6 * n)
 
     def ring(part):
         axis, chunk, rl, rf, sem = rings[part]
@@ -237,10 +244,17 @@
 
     steps = {part: ring(part) for part in rings}
 
+    def ring_far(part):
+        for k in (0, 1):
+            steps[part][k][0].start()
+
+    def ring_near(part):
+        for k in (0, 1):
+            steps[part][k][1].start()
+
     def ring_start(part):
-        for which in (0, 1):
-            for k in (0, 1):
-                steps[part][k][which].start()
+        ring_far(part)
+        ring_near(part)
 
     def ring_relay(part):
         for k in (0, 1):
@@ -344,15 +358,17 @@
     columns(1, D + T, D)
     for n in (0, 1, 2, 5, 6, 7):
         filt(n)
-    ring_start("B1")
-    ring_start("C1")
+    late = ("B1", "C1", "B2", "C2")
+    for part in late:
+        ring_far(part)
     ring_relay("C0")
 
     @pl.when(c == 0)
     def _():
         for n in range(8):
             pf[n // 2, 576 * (n % 2):576 * (n % 2 + 1)] = rows_of(576 * n, 576, 256, 384).astype(BF)
-        ring_start("F")
+        ring_far("F0")
+        ring_far("F1")
 
     def du(lo, hi):
         @pl.loop(lo, hi)
@@ -430,14 +446,25 @@
     @pl.when(c == 1)
     def _():
         ring_relay("G")
-
-    du(0, 3)
-    ring_relay("B1")
-    ring_relay("C1")
+        du(0, 1)
+
+    for part in late:
+        ring_near(part)
 
     @pl.when(c == 0)
     def _():
-        ring_relay("F")
+        du(0, 1)
+        ring_near("F0")
+        ring_near("F1")
+
+    du(1, 3)
+    for part in late:
+        ring_relay(part)
+
+    @pl.when(c == 0)
+    def _():
+        ring_relay("F0")
+        ring_relay("F1")
     ring_end("A")
     for h in range(2):
         sa[320 * h:320 * (h + 1)] = up32(pa[y, 320 * h:320 * (h + 1)]) + up32(rfa[0, 1 - h]) + up32(rfa[1, h])
@@ -449,15 +476,16 @@
     s2f[288:304] = jnp.zeros((16, 128), F32)
     s2b[288:304] = jnp.zeros((16, 128), F32)
     s2c[288:304] = jnp.zeros((16, 128), F32)
-    def sum_bc(p, i, rf, to):
-        for first, off, rows in ((0, 0, 144), (288, 144, 432)):
+    def sum_pieces(p, i, rf, to, pieces):
+        for first, off, rows in pieces:
             for h in range(2):
                 r, f = pl.ds(first + rows * h, rows), pl.ds(off, rows)
                 to[r] = up32(p[i, r]) + up32(rf[0, 1 - h, f]) + up32(rf[1, h, f])
 
     ring_end("B0")
     ring_end("B1")
-    sum_bc(pb, x, rfb, sb)
+    ring_end("B2")
+    sum_pieces(pb, x, rfb, sb, PIECES)
     for h in range(2):
         for zz in range(4):
             lo = 576 * h + 72 * zz
@@ -467,22 +495,19 @@
 
     ring_end("C0")
     ring_end("C1")
-    sum_bc(pc, z, rfc, sc)
+    ring_end("C2")
+    sum_pieces(pc, z, rfc, sc, PIECES)
     for yy in range(4):
         for xp in range(2):
             lo = row_c(yy, xp)
             qc[yy, 144 * xp:144 * (xp + 1)] = sc[lo:lo + 144].astype(BF)
     begin(sec_c)
 
-    def sum_f(rows):
-        for h in range(2):
-            r = pl.ds(rows * h, rows)
-            sf[r] = up32(pf[y, r]) + up32(rff[0, 1 - h, 0:rows]) + up32(rff[1, h, 0:rows])
-
     @pl.when(c == 0)
     def _():
-        ring_end("F")
-        sum_f(576)
+        ring_end("F0")
+        ring_end("F1")
+        sum_pieces(pf, y, rff, sf, PIECES_F)
         for xx in range(4):
             qf[xx] = sf[288 * xx:288 * (xx + 1)].astype(BF)
         begin(sec_f)
@@ -490,7 +515,7 @@
     @pl.when(c == 1)
     def _():
         ring_end("G")
-        sum_f(320)
+        sum_pieces(pf, y, rff, sf, ((0, 0, 320),))
         pairs(qf, sf)
         begin(sec_g)
 
@@ -568,14 +593,13 @@
                 steps[part][k][w].wait_send()
 
     ring_left("A")
-    ring_left("B0")
-    ring_left("B1")
-    ring_left("C0")
-    ring_left("C1")
+    for part in ("B0", "C0") + late:
+        ring_left(part)
 
     @pl.when(c == 0)
     def _():
-        ring_left("F")
+        ring_left("F0")
+        ring_left("F1")
         for cp in sec_f:
             cp.wait_send()
 

time: 49.5 us -> 49.3 us (level)
  no operation moved by 1% of the time
where the time goes in v4:
time: 49.3 us; the launch traced here: 49.1 us
  Pallas kernels  48.5 us (98%)
  between operations  0.64 us (1%)
    pallas_call x1, Pallas kernels, shards(): pl.pallas_call(kernel, name='block_backward', out_shape=shapes, in_specs=...  46.4 us
    pallas_call x1, Pallas kernels, shards(): pl.pallas_call(finish, name='hand_out', out_shape=shapes, in_specs=[anywh...  2.1 us

profile of v4, /device:TPU:1, one launch (start us, length us, event | category | flops | bytes accessed | tf_op | source)
XLA Modules:
  0.0 49.1 jit_solution(6169882341415022229)
XLA Ops:
  0.6 46.4 %block_backward.1 = (bf16[1,256,1536]{2,1,0:T(8,128)(2,1)}, f32[36,640]{1,0:T(8,128)}, f32[5,1536]{1,0:T(8,128)}) custom-call(bf16[1,256,1536]{2,1,0:T(8,128)(2,1)} %x_hbm.1, bf16[1,256,1536]{2,1,0:T(8,128)(2,1)} %cot_hbm.1, bf16[4608,640]{1,0:T(8,128)(2,1)} %fw_hbm.1, bf16[640,1536]{1,0:T(8,128)(2,1)} %pw_hbm.1), custom_call_target="tpu_custom_call" | custom-call | flops 5600000000 | bytes 12000000 | tf_op jit(solution)/shard_map/block_backward/pallas_call | solution.py:655
  47.0 2.1 %hand_out.1 = (bf16[1,256,1536]{2,1,0:T(8,128)(2,1)}, f32[36,640]{1,0:T(8,128)}, f32[5,1536]{1,0:T(8,128)}) custom-call(bf16[1,256,1536]{2,1,0:T(8,128)(2,1)} %get-tuple-element.6.refs_0_, f32[36,640]{1,0:T(8,128)} %get-tuple-element.7.refs_1_, f32[5,1536]{1,0:T(8,128)} %get-tuple-element.8.refs_2_), custom_call_target="tpu_custom_call" | custom-call | tf_op jit(solution)/shard_map/hand_out/pallas_call | solution.py:666

commit v5 on v4

--- a/solution.py
+++ b/solution.py
@@ -24,7 +24,7 @@
 
 
 PIECES = ((0, 0, 144), (288, 144, 224), (736, 368, 208))
-PIECES_F = ((0, 0, 288), (576, 288, 288))
+PIECES_F = ((0, 0, 144), (288, 144, 144))
 
 
 def slot_b(xx, yy):
@@ -218,8 +218,7 @@
         return r.at[..., pl.ds(first, rows), :]
 
     rings = {
-        "A": ("y", flat(pa, 0, 320), rla, rfa, S_P1),
-        "G": ("y", flat(pf, 0, 320), cut(rlf, 0, 320), cut(rff, 0, 320), S_P1 + 6),
+        "A": ("y", flat(pa, 0, 480), rla, rfa, S_P1),
     }
     for n, (first, off, rows) in enumerate(PIECES_F):
         rings[f"F{n}"] = ("y", flat(pf, first, rows), cut(rlf, off, rows), cut(rff, off, rows), S_P1 + 6 + 6 * n)
@@ -278,15 +277,9 @@
 
     sib_c.wait_recv()
     sib_g.wait_recv()
-    for n in range(2):
-        proj(pa, 512 * c + 256 * n, n)
-    ring_start("A")
-
-    @pl.when(c == 1)
-    def _():
-        for n in range(2):
-            proj(pf, 1024 + 256 * n, n)
-        ring_start("G")
+    for n in range(3):
+        proj(pa, 768 * c + 256 * n, n)
+    ring_far("A")
 
     def columns(s, first, rows):
         r = pl.ds(first, rows)
@@ -321,6 +314,14 @@
                 [acc[72 * zz:72 * zz + 72, 128:256], acc[288 + 72 * zz:360 + 72 * zz, 128:256]],
                 axis=0).astype(BF)
 
+    def filt_last(groups):
+        for core in range(2):
+            @pl.when(c == core)
+            def _():
+                for n in groups:
+                    pf[n // 4, 144 * (n % 4):144 * (n % 4 + 1)] = (
+                        rows_of(288 * n + 144 * core, 144, 256, 384).astype(BF))
+
     columns(0, D, T)
     sib_u.wait_recv()
     sib_d.wait_recv()
@@ -328,6 +329,8 @@
     filt(3)
     filt(4)
     ring_start("B0")
+    ring_near("A")
+    filt_last((6, 7, 8, 9))
     @pl.when(has_prev)
     def _():
         dz_up.wait_recv()
@@ -350,25 +353,25 @@
     columns(0, 0, D)
     columns(0, D + T, D)
     ring_start("C0")
-    ring_relay("A")
     ring_relay("B0")
     sib_lo.wait_recv()
     sib_hi.wait_recv()
     columns(1, 0, D)
     columns(1, D + T, D)
-    for n in (0, 1, 2, 5, 6, 7):
+    late = ("B1", "C1", "B2", "C2")
+    for n in (0, 1, 2, 5):
         filt(n)
-    late = ("B1", "C1", "B2", "C2")
-    for part in late:
-        ring_far(part)
+    ring_far("B1")
+    ring_far("C1")
+    ring_relay("A")
+    for n in (6, 7):
+        filt(n)
+    ring_far("B2")
+    ring_far("C2")
     ring_relay("C0")
-
-    @pl.when(c == 0)
-    def _():
-        for n in range(8):
-            pf[n // 2, 576 * (n % 2):576 * (n % 2 + 1)] = rows_of(576 * n, 576, 256, 384).astype(BF)
-        ring_far("F0")
-        ring_far("F1")
+    filt_last((0, 1, 2, 3, 4, 5, 10, 11, 12, 13, 14, 15))
+    ring_far("F0")
+    ring_far("F1")
 
     def du(lo, hi):
         @pl.loop(lo, hi)
@@ -387,8 +390,6 @@
 
     sec_a = second("x", qa, rqa, S_P2)
     sec_f = second("x", qf, rqf, S_P2 + 3)
-    sec_g = [remote(qf.at[(x + d) % 4, pl.ds(0, 160)], rqf.at[d - 1, pl.ds(0, 160)],
-                    (S_P2 + 2 + d, S_P2 + 2 + d), at("x", d, c)) for d in (1, 2, 3)]
     sec_b = second("z", qb, rqb, S_P2 + 6)
     sec_c = second("y", qc, rqc, S_P2 + 9)
 
@@ -408,7 +409,22 @@
         return out, wait
 
     thr_a = third("z", ta, rta, S_P3)
-    thr_f = third("z", tf, rtf, S_P3 + 8)
+    s_f = S_P3 + 8
+    half = z // 2
+    to_f = [[remote(tf.at[(z + d) % 4, cc], rtf.at[c, d], (s_f + 4 * cc + d, s_f + 4 * c + d), at("z", d, cc))
+             for cc in (0, 1)] for d in (1, 2, 3)]
+    to_sib = remote(tf.at[z, o], rtf.at[c, 0], (s_f + 4 * o, s_f + 4 * c), sibling)
+    from_f = [remote(tf.at[0, 0], rtf.at[half, d], (s_f + 4 * half + d, s_f + 4 * half + d), sibling)
+              for d in (1, 2, 3)]
+    from_sib = remote(tf.at[0, 0], rtf.at[o, 0], (s_f + 4 * o, s_f + 4 * o), sibling)
+
+    def each_to_f(do):
+        for d in (1, 2, 3):
+            @pl.when(((z + d) % 4) // 2 == c)
+            def _():
+                for cp in to_f[d - 1]:
+                    do(cp)
+
     thr_b = third("y", tb, rtb, S_P3 + 16)
     thr_c = third("x", tc, rtc, S_P3 + 24)
 
@@ -417,7 +433,7 @@
             cp.start()
 
     def pairs(q, s):
-        for p in range(2):
+        for p in range(3):
             for xx in range(4):
                 lo = 320 * p + 40 * xx
                 q[xx, 80 * p:80 * (p + 1)] = jnp.concatenate(
@@ -436,44 +452,27 @@
                 t[owner, cc] = s2[lo:lo + 48].astype(BF)
 
     def fives(s2, t):
-        for p in range(2):
+        for p in range(3):
             for n in range(4):
                 for cc in range(2):
                     lo = 80 * p + 10 * n + 5 * cc
                     t[n, cc, 16 * p:16 * (p + 1)] = jnp.concatenate(
                         [s2[lo:lo + 8], s2[lo + 40:lo + 48]], axis=0).astype(BF)
 
-    @pl.when(c == 1)
-    def _():
-        ring_relay("G")
-        du(0, 1)
-
+    du(0, 1)
     for part in late:
         ring_near(part)
-
-    @pl.when(c == 0)
-    def _():
-        du(0, 1)
-        ring_near("F0")
-        ring_near("F1")
-
+    ring_near("F0")
+    ring_near("F1")
     du(1, 3)
     for part in late:
         ring_relay(part)
-
-    @pl.when(c == 0)
-    def _():
-        ring_relay("F0")
-        ring_relay("F1")
-    ring_end("A")
-    for h in range(2):
-        sa[320 * h:320 * (h + 1)] = up32(pa[y, 320 * h:320 * (h + 1)]) + up32(rfa[0, 1 - h]) + up32(rfa[1, h])
-    pairs(qa, sa)
-    begin(sec_a)
-
-
-    s2a[160:168] = jnp.zeros((8, 128), F32)
-    s2f[288:304] = jnp.zeros((16, 128), F32)
+    ring_relay("F0")
+    ring_relay("F1")
+
+
+    s2a[240:248] = jnp.zeros((8, 128), F32)
+    s2f[144:160] = jnp.zeros((16, 128), F32)
     s2b[288:304] = jnp.zeros((16, 128), F32)
     s2c[288:304] = jnp.zeros((16, 128), F32)
     def sum_pieces(p, i, rf, to, pieces):
@@ -481,6 +480,11 @@
             for h in range(2):
                 r, f = pl.ds(first + rows * h, rows), pl.ds(off, rows)
                 to[r] = up32(p[i, r]) + up32(rf[0, 1 - h, f]) + up32(rf[1, h, f])
+
+    ring_end("A")
+    sum_pieces(pa, y, rfa, sa, ((0, 0, 480),))
+    pairs(qa, sa)
+    begin(sec_a)
 
     ring_end("B0")
     ring_end("B1")
@@ -503,26 +507,16 @@
             qc[yy, 144 * xp:144 * (xp + 1)] = sc[lo:lo + 144].astype(BF)
     begin(sec_c)
 
-    @pl.when(c == 0)
-    def _():
-        ring_end("F0")
-        ring_end("F1")
-        sum_pieces(pf, y, rff, sf, PIECES_F)
-        for xx in range(4):
-            qf[xx] = sf[288 * xx:288 * (xx + 1)].astype(BF)
-        begin(sec_f)
-
-    @pl.when(c == 1)
-    def _():
-        ring_end("G")
-        sum_pieces(pf, y, rff, sf, ((0, 0, 320),))
-        pairs(qf, sf)
-        begin(sec_g)
-
+    ring_end("F0")
+    ring_end("F1")
+    sum_pieces(pf, y, rff, sf, PIECES_F)
+    for xx in range(4):
+        qf[xx] = sf[144 * xx:144 * (xx + 1)].astype(BF)
+    begin(sec_f)
     du(3, 6)
     store_ig = local(ig, ig_hbm.at[0], 6)
     store_ig.start()
-    gather(sec_a, qa, rqa, x, s2a, 160)
+    gather(sec_a, qa, rqa, x, s2a, 240)
     fives(s2a, ta)
     begin(thr_a[0])
     rta[c, 0] = ta[z, c]
@@ -536,22 +530,17 @@
         begin(thr[0])
         rt[c, 0] = t[i, c]
 
-    @pl.when(c == 0)
-    def _():
-        gather(sec_f, qf, rqf, x, s2f, 288)
-        rows36(s2f, tf)
-
-    @pl.when(c == 1)
-    def _():
-        gather(sec_g, qf, rqf, x, s2f, 160)
-        s2f[160:168] = jnp.zeros((8, 128), F32)
-        fives(s2f, tf)
-        for n in range(4):
-            for cc in range(2):
-                tf[n, cc, 32:48] = jnp.zeros((16, 128), BF)
-
-    begin(thr_f[0])
-    rtf[c, 0] = tf[z, c]
+    gather(sec_f, qf, rqf, x, s2f, 144)
+    for n in range(2):
+        for cc in range(2):
+            lo = 72 * n + 36 * cc
+            tf[2 * c + n, cc] = s2f[lo:lo + 48].astype(BF)
+    each_to_f(lambda cp: cp.start())
+
+    @pl.when(half == c)
+    def _():
+        to_sib.start()
+        rtf[c, 0] = tf[z, c]
 
     scale = 1.0 / (4 * 8192) ** 0.5
 
@@ -560,20 +549,22 @@
             cp.wait_recv()
         return [(up32(rt[s, 0]) + up32(rt[s, 1]) + up32(rt[s, 2]) + up32(rt[s, 3])) * scale for s in range(2)]
 
-    def put_proj(v, first):
-        for b in range(4):
-            po_ref[:, 128 * (first + b):128 * (first + b + 1)] = v[8 * b:8 * b + 5]
-
-    low, high = total(thr_a, rta)
-    put_proj(low, 0)
-    put_proj(high, 4)
+    for s, v in enumerate(total(thr_a, rta)):
+        for b in range(6):
+            po_ref[:, 768 * s + 128 * b:768 * s + 128 * (b + 1)] = v[8 * b:8 * b + 5]
     for s, v in enumerate(total(thr_b, rtb)):
         fo_ref[:, 256 * s:256 * s + 128] = v[0:36]
     for s, v in enumerate(total(thr_c, rtc)):
         fo_ref[:, 256 * s + 128:256 * s + 256] = v[0:36]
-    low, high = total(thr_f, rtf)
-    fo_ref[:, 512:640] = low[0:36]
-    put_proj(high, 8)
+    for cp in from_f:
+        cp.wait_recv()
+
+    @pl.when(half != c)
+    def _():
+        from_sib.wait_recv()
+
+    last = up32(rtf[half, 0]) + up32(rtf[half, 1]) + up32(rtf[half, 2]) + up32(rtf[half, 3])
+    fo_ref[:, 512:640] = (last * scale)[0:36]
 
     @pl.when(has_next)
     def _():
@@ -593,23 +584,16 @@
                 steps[part][k][w].wait_send()
 
     ring_left("A")
-    for part in ("B0", "C0") + late:
+    for part in ("B0", "C0", "F0", "F1") + late:
         ring_left(part)
 
-    @pl.when(c == 0)
-    def _():
-        ring_left("F0")
-        ring_left("F1")
-        for cp in sec_f:
-            cp.wait_send()
-
-    @pl.when(c == 1)
-    def _():
-        ring_left("G")
-        for cp in sec_g:
-            cp.wait_send()
-
-    for cp in sec_a + sec_b + sec_c + thr_a[0] + thr_f[0] + thr_b[0] + thr_c[0]:
+    each_to_f(lambda cp: cp.wait_send())
+
+    @pl.when(half == c)
+    def _():
+        to_sib.wait_send()
+
+    for cp in sec_a + sec_f + sec_b + sec_c + thr_a[0] + thr_b[0] + thr_c[0]:
         cp.wait_send()
     store_ig.wait()
 
@@ -635,15 +619,15 @@
         v((T, C), BF), v((T, C), BF), v((2, C, T), BF), v((2 * T, C), BF), v((3 * C, H), BF), v((H, C), BF),
         v((2, D, H), BF), v((2, D, H), BF), v((T, H), F32), v((T, H), F32), v((T, H), BF),
         v((2, H, T), BF), v((2, T + 2 * D, H), BF), v((2, T + 2 * D, 384), BF),
-        v((4, 640, 128), BF), v((4, 1152, 128), BF), v((4, 1152, 128), BF), v((4, 1152, 128), BF),
-        v((2, 320, 128), BF), v((2, 576, 128), BF), v((2, 576, 128), BF), v((2, 576, 128), BF),
-        v((2, 2, 320, 128), BF), v((2, 2, 576, 128), BF), v((2, 2, 576, 128), BF), v((2, 2, 576, 128), BF),
-        v((640, 128), F32), v((1152, 128), F32), v((1152, 128), F32), v((1152, 128), F32),
-        v((4, 160, 128), BF), v((4, 288, 128), BF), v((4, 288, 128), BF), v((4, 288, 128), BF),
-        v((3, 160, 128), BF), v((3, 288, 128), BF), v((3, 288, 128), BF), v((3, 288, 128), BF),
-        v((168, 128), F32), v((304, 128), F32), v((304, 128), F32), v((304, 128), F32),
-        v((4, 2, 32, 128), BF), v((4, 2, 48, 128), BF), v((4, 2, 48, 128), BF), v((4, 2, 48, 128), BF),
-        v((2, 4, 32, 128), BF), v((2, 4, 48, 128), BF), v((2, 4, 48, 128), BF), v((2, 4, 48, 128), BF),
+        v((4, 960, 128), BF), v((4, 576, 128), BF), v((4, 1152, 128), BF), v((4, 1152, 128), BF),
+        v((2, 480, 128), BF), v((2, 288, 128), BF), v((2, 576, 128), BF), v((2, 576, 128), BF),
+        v((2, 2, 480, 128), BF), v((2, 2, 288, 128), BF), v((2, 2, 576, 128), BF), v((2, 2, 576, 128), BF),
+        v((960, 128), F32), v((576, 128), F32), v((1152, 128), F32), v((1152, 128), F32),
+        v((4, 240, 128), BF), v((4, 144, 128), BF), v((4, 288, 128), BF), v((4, 288, 128), BF),
+        v((3, 240, 128), BF), v((3, 144, 128), BF), v((3, 288, 128), BF), v((3, 288, 128), BF),
+        v((248, 128), F32), v((160, 128), F32), v((304, 128), F32), v((304, 128), F32),
+        v((4, 2, 48, 128), BF), v((4, 2, 48, 128), BF), v((4, 2, 48, 128), BF), v((4, 2, 48, 128), BF),
+        v((2, 4, 48, 128), BF), v((2, 4, 48, 128), BF), v((2, 4, 48, 128), BF), v((2, 4, 48, 128), BF),
         v((T, C), BF),
         pltpu.SemaphoreType.DMA((8,)), pltpu.SemaphoreType.DMA((N_SEM,)), pltpu.SemaphoreType.DMA((N_SEM,)),
     ]

time: 49.3 us -> 48.9 us (level)
  no operation moved by 1% of the time
where the time goes in v5:
time: 48.9 us; the launch traced here: 48.8 us
  Pallas kernels  48.1 us (98%)
  between operations  0.64 us (1%)
    pallas_call x1, Pallas kernels, shards(): pl.pallas_call(kernel, name='block_backward', out_shape=shapes, in_specs=...  46 us
    pallas_call x1, Pallas kernels, shards(): pl.pallas_call(finish, name='hand_out', out_shape=shapes, in_specs=[anywh...  2.1 us

profile of v5, /device:TPU:1, one launch (start us, length us, event | category | flops | bytes accessed | tf_op | source)
XLA Modules:
  0.0 48.8 jit_solution(17799109020369750128)
XLA Ops:
  0.6 46.0 %block_backward.1 = (bf16[1,256,1536]{2,1,0:T(8,128)(2,1)}, f32[36,640]{1,0:T(8,128)}, f32[5,1536]{1,0:T(8,128)}) custom-call(bf16[1,256,1536]{2,1,0:T(8,128)(2,1)} %x_hbm.1, bf16[1,256,1536]{2,1,0:T(8,128)(2,1)} %cot_hbm.1, bf16[4608,640]{1,0:T(8,128)(2,1)} %fw_hbm.1, bf16[640,1536]{1,0:T(8,128)(2,1)} %pw_hbm.1), custom_call_target="tpu_custom_call" | custom-call | flops 5600000000 | bytes 12000000 | tf_op jit(solution)/shard_map/block_backward/pallas_call | solution.py:639
  46.7 2.1 %hand_out.1 = (bf16[1,256,1536]{2,1,0:T(8,128)(2,1)}, f32[36,640]{1,0:T(8,128)}, f32[5,1536]{1,0:T(8,128)}) custom-call(bf16[1,256,1536]{2,1,0:T(8,128)(2,1)} %get-tuple-element.6.refs_0_, f32[36,640]{1,0:T(8,128)} %get-tuple-element.7.refs_1_, f32[5,1536]{1,0:T(8,128)} %get-tuple-element.8.refs_2_), custom_call_target="tpu_custom_call" | custom-call | tf_op jit(solution)/shard_map/hand_out/pallas_call | solution.py:650

commit v6 on v5

--- a/solution.py
+++ b/solution.py
@@ -386,7 +386,7 @@
 
     def second(axis, q, rq, sem):
         return [remote(q.at[(pos[axis] + d) % 4], rq.at[d - 1], (sem + d - 1, sem + d - 1), at(axis, d, c))
-                for d in (1, 2, 3)]
+                for d in (1, 3, 2)]
 
     sec_a = second("x", qa, rqa, S_P2)
     sec_f = second("x", qf, rqf, S_P2 + 3)
@@ -396,7 +396,7 @@
     def third(axis, t, rt, sem):
         i = pos[axis]
         out = []
-        for d in (2, 1, 3):
+        for d in (1, 3, 2):
             for cc in (0, 1):
                 out.append(remote(t.at[(i + d) % 4, cc], rt.at[c, d],
                                   (sem + 4 * cc + d, sem + 4 * c + d), at(axis, d, cc)))

time: 48.9 us -> 49 us (level)
  no operation moved by 1% of the time
where the time goes in v6:
time: 49 us; the launch traced here: 48.9 us
  Pallas kernels  48.2 us (98%)
  between operations  0.64 us (1%)
    pallas_call x1, Pallas kernels, shards(): pl.pallas_call(kernel, name='block_backward', out_shape=shapes, in_specs=...  46.1 us
    pallas_call x1, Pallas kernels, shards(): pl.pallas_call(finish, name='hand_out', out_shape=shapes, in_specs=[anywh...  2.1 us

profile of v6, /device:TPU:1, one launch (start us, length us, event | category | flops | bytes accessed | tf_op | source)
XLA Modules:
  0.0 48.9 jit_solution(5969927800935540242)
XLA Ops:
  0.6 46.1 %block_backward.1 = (bf16[1,256,1536]{2,1,0:T(8,128)(2,1)}, f32[36,640]{1,0:T(8,128)}, f32[5,1536]{1,0:T(8,128)}) custom-call(bf16[1,256,1536]{2,1,0:T(8,128)(2,1)} %x_hbm.1, bf16[1,256,1536]{2,1,0:T(8,128)(2,1)} %cot_hbm.1, bf16[4608,640]{1,0:T(8,128)(2,1)} %fw_hbm.1, bf16[640,1536]{1,0:T(8,128)(2,1)} %pw_hbm.1), custom_call_target="tpu_custom_call" | custom-call | flops 5600000000 | bytes 12000000 | tf_op jit(solution)/shard_map/block_backward/pallas_call | solution.py:639
  46.8 2.1 %hand_out.1 = (bf16[1,256,1536]{2,1,0:T(8,128)(2,1)}, f32[36,640]{1,0:T(8,128)}, f32[5,1536]{1,0:T(8,128)}) custom-call(bf16[1,256,1536]{2,1,0:T(8,128)(2,1)} %get-tuple-element.6.refs_0_, f32[36,640]{1,0:T(8,128)} %get-tuple-element.7.refs_1_, f32[5,1536]{1,0:T(8,128)} %get-tuple-element.8.refs_2_), custom_call_target="tpu_custom_call" | custom-call | tf_op jit(solution)/shard_map/hand_out/pallas_call | solution.py:650

commit v7 on v5

--- a/solution.py
+++ b/solution.py
@@ -459,12 +459,12 @@
                     t[n, cc, 16 * p:16 * (p + 1)] = jnp.concatenate(
                         [s2[lo:lo + 8], s2[lo + 40:lo + 48]], axis=0).astype(BF)
 
-    du(0, 1)
+    du(0, 2)
     for part in late:
         ring_near(part)
     ring_near("F0")
     ring_near("F1")
-    du(1, 3)
+    du(2, 3)
     for part in late:
         ring_relay(part)
     ring_relay("F0")

time: 48.9 us -> 49.6 us (1.014)
  Pallas kernels: 48.1 us -> 48.8 us
    pallas_call x1, Pallas kernels: 46 us -> 46.8 us  [shards(): pl.pallas_call(kernel, name='block_backward', out_shape=shapes, in_specs=...]
where the time goes in v7:
time: 49.6 us; the launch traced here: 49.5 us
  Pallas kernels  48.8 us (98%)
  between operations  0.64 us (1%)
    pallas_call x1, Pallas kernels, shards(): pl.pallas_call(kernel, name='block_backward', out_shape=shapes, in_specs=...  46.8 us
    pallas_call x1, Pallas kernels, shards(): pl.pallas_call(finish, name='hand_out', out_shape=shapes, in_specs=[anywh...  2.1 us

profile of v7, /device:TPU:1, one launch (start us, length us, event | category | flops | bytes accessed | tf_op | source)
XLA Modules:
  0.0 49.5 jit_solution(5919066993818311724)
XLA Ops:
  0.6 46.8 %block_backward.1 = (bf16[1,256,1536]{2,1,0:T(8,128)(2,1)}, f32[36,640]{1,0:T(8,128)}, f32[5,1536]{1,0:T(8,128)}) custom-call(bf16[1,256,1536]{2,1,0:T(8,128)(2,1)} %x_hbm.1, bf16[1,256,1536]{2,1,0:T(8,128)(2,1)} %cot_hbm.1, bf16[4608,640]{1,0:T(8,128)(2,1)} %fw_hbm.1, bf16[640,1536]{1,0:T(8,128)(2,1)} %pw_hbm.1), custom_call_target="tpu_custom_call" | custom-call | flops 5600000000 | bytes 12000000 | tf_op jit(solution)/shard_map/block_backward/pallas_call | solution.py:639
  47.4 2.1 %hand_out.1 = (bf16[1,256,1536]{2,1,0:T(8,128)(2,1)}, f32[36,640]{1,0:T(8,128)}, f32[5,1536]{1,0:T(8,128)}) custom-call(bf16[1,256,1536]{2,1,0:T(8,128)(2,1)} %get-tuple-element.6.refs_0_, f32[36,640]{1,0:T(8,128)} %get-tuple-element.7.refs_1_, f32[5,1536]{1,0:T(8,128)} %get-tuple-element.8.refs_2_), custom_call_target="tpu_custom_call" | custom-call | tf_op jit(solution)/shard_map/hand_out/pallas_call | solution.py:650
